TPU v7x, 256 devices: a whole 4x4x8 slice. The times are simulated.
256 devices in a mesh: dp: 8 (over y, core), seq: 32 (over x, z).
Axes of the slice: x: 4, y: 4, z: 8, core: 2. Of those that a mesh axis runs over, the one named last changes fastest.
Arguments:
- queries: bfloat16 [8, 16384, 640], P('dp', 'seq'), may hold values from -10 to 10
- keys: bfloat16 [8, 16384, 640], P('dp', 'seq'), may hold values from -4 to 4
- values: bfloat16 [8, 16384, 640], P('dp', 'seq'), may hold values from -6 to 6
- upstream: bfloat16 [8, 16384, 1280], P('dp', 'seq'), may hold values from -24 to 24
- out_weight: bfloat16 [640, 1280], replicated, may hold values from -0.25 to 0.25
- visible: int32 [8, 16384], P('dp', 'seq'), may hold values from 0 to 1, as said below
Outputs:
- grad_queries: bfloat16 [8, 16384, 640], P('dp', 'seq')
- grad_keys: bfloat16 [8, 16384, 640], P('dp', 'seq')
- grad_values: bfloat16 [8, 16384, 640], P('dp', 'seq')
- grad_weight: float32 [640, 1280], P('seq')
Inputs may be any that keep to these rules, and one draw needn't show every extreme that they name: In every scene, the patches of the devices 2 j and 2 j + 1 along seq (512 each, in order) hold together at most 144 visible ones; in every scene one device's patches hold exactly 144 visible ones and those of its partner none.
All inputs are finite; a program needn't handle non-finite values.
Results may differ from a plain program's by a relative error of at most 0.014.
Values may be sent and summed in bfloat16 or wider, within the bound.
A program may use at most 128 MiB of HBM per device.

v0:
```python
import jax
import jax.numpy as jnp
from jax import lax
from jax.sharding import PartitionSpec as P

HEAD_DIM = 80
VIS_MAX = 144


NEGATIVE_FILL = -1e30


def split_heads(matrix, head_count):
    return matrix.reshape(matrix.shape[0], head_count, -1).transpose(1, 0, 2)


def merge_heads(stacked):
    return stacked.transpose(1, 0, 2).reshape(stacked.shape[1], -1)


def per_device(queries, keys, values, upstream, out_weight, visible):
    row_flags = visible[0]
    patch_count = row_flags.shape[0]
    feature_width = queries.shape[2]
    head_count = feature_width // HEAD_DIM
    score_scale = HEAD_DIM ** (-0.5)
    vis_count = jnp.sum(row_flags)
    row_rank = jnp.cumsum(row_flags) - 1
    slot_index = jnp.where(row_flags == 1, row_rank, VIS_MAX)
    source_rows = (
        jnp.zeros((VIS_MAX + 1,), jnp.int32)
        .at[slot_index]
        .set(jnp.arange(patch_count, dtype=jnp.int32))[:VIS_MAX]
    )
    payload = jnp.concatenate([queries[0], keys[0], values[0], upstream[0]], axis=1)
    taken = jnp.take(payload, source_rows, axis=0)
    packed = jnp.where((jnp.arange(VIS_MAX) < vis_count)[:, None], taken, jnp.zeros_like(taken))
    capacity = packed.shape[0]
    query_rows = packed[:, :feature_width]
    key_rows = packed[:, feature_width : 2 * feature_width]
    value_rows = packed[:, 2 * feature_width : 3 * feature_width]
    upstream_rows = packed[:, 3 * feature_width :]
    live_rows = jnp.arange(capacity) < vis_count
    grad_out = lax.dot_general(
        upstream_rows, out_weight, (((1,), (1,)), ((), ())), preferred_element_type=jnp.float32
    ).astype(jnp.bfloat16)
    all_keys, all_values, all_live = (
        lax.all_gather(key_rows, "seq", axis=0, tiled=True),
        lax.all_gather(value_rows, "seq", axis=0, tiled=True),
        lax.all_gather(live_rows.astype(jnp.bfloat16), "seq", axis=0, tiled=True),
    )
    key_mask = all_live > 0

    def own_rows(parts):
        query_head, key_head, value_head, grad_head = parts
        scores = (
            lax.dot_general(
                query_head, key_head, (((1,), (1,)), ((), ())), preferred_element_type=jnp.float32
            )
            * score_scale
        )
        scores = jnp.where(key_mask[None, :], scores, NEGATIVE_FILL)
        row_max = jnp.max(scores, axis=1, keepdims=True)
        log_total = row_max + jnp.log(jnp.sum(jnp.exp(scores - row_max), axis=1, keepdims=True))
        probability = jnp.exp(scores - log_total)
        weights = probability.astype(jnp.bfloat16)
        attended = jnp.dot(weights, value_head, preferred_element_type=jnp.float32).astype(
            jnp.bfloat16
        )
        row_delta = jnp.sum(
            grad_head.astype(jnp.float32) * attended.astype(jnp.float32), axis=1, keepdims=True
        )
        grad_prob = lax.dot_general(
            grad_head, value_head, (((1,), (1,)), ((), ())), preferred_element_type=jnp.float32
        )
        grad_score = (probability * (grad_prob - row_delta) * score_scale).astype(jnp.bfloat16)
        grad_query = jnp.dot(grad_score, key_head, preferred_element_type=jnp.float32).astype(
            jnp.bfloat16
        )
        return (attended, grad_query, log_total[:, 0], row_delta[:, 0])

    attended, grad_query, log_total, row_delta = lax.map(
        own_rows,
        (
            split_heads(query_rows, head_count),
            split_heads(all_keys, head_count),
            split_heads(all_values, head_count),
            split_heads(grad_out, head_count),
        ),
    )
    all_totals, all_deltas = (
        lax.all_gather(log_total, "seq", axis=1, tiled=True),
        lax.all_gather(row_delta, "seq", axis=1, tiled=True),
    )
    own_keys = split_heads(key_rows, head_count)
    own_values = split_heads(value_rows, head_count)
    query_piece = lax.all_gather(query_rows, "seq", axis=0, tiled=True)
    grad_piece = lax.all_gather(grad_out, "seq", axis=0, tiled=True)

    def one_head(parts):
        query_head, grad_head, total_head, delta_head, key_head, value_head = parts
        scores = (
            lax.dot_general(
                query_head, key_head, (((1,), (1,)), ((), ())), preferred_element_type=jnp.float32
            )
            * score_scale
        )
        scores = jnp.where(live_rows[None, :], scores, NEGATIVE_FILL)
        probability = jnp.exp(scores - total_head[:, None])
        weights = probability.astype(jnp.bfloat16)
        grad_prob = lax.dot_general(
            grad_head, value_head, (((1,), (1,)), ((), ())), preferred_element_type=jnp.float32
        )
        grad_score = (probability * (grad_prob - delta_head[:, None]) * score_scale).astype(
            jnp.bfloat16
        )
        key_term = lax.dot_general(
            grad_score, query_head, (((0,), (0,)), ((), ())), preferred_element_type=jnp.float32
        )
        value_term = lax.dot_general(
            weights, grad_head, (((0,), (0,)), ((), ())), preferred_element_type=jnp.float32
        )
        return (key_term, value_term)

    key_terms, value_terms = lax.map(
        one_head,
        (
            split_heads(query_piece, head_count),
            split_heads(grad_piece, head_count),
            all_totals,
            all_deltas,
            own_keys,
            own_values,
        ),
    )
    attended_rows = merge_heads(attended)
    share = feature_width // lax.axis_size("seq")
    weight_term = lax.dot_general(
        attended_rows, upstream_rows, (((0,), (0,)), ((), ())), preferred_element_type=jnp.float32
    )
    weight_whole = lax.psum(weight_term, ("dp", "seq"))
    grad_weight = lax.dynamic_slice_in_dim(weight_whole, lax.axis_index("seq") * share, share, 0)
    results = jnp.concatenate(
        [
            merge_heads(grad_query),
            merge_heads(key_terms).astype(jnp.bfloat16),
            merge_heads(value_terms).astype(jnp.bfloat16),
        ],
        axis=1,
    )
    placed = jnp.take(results, jnp.clip(row_rank, 0, VIS_MAX - 1), axis=0)
    placed = jnp.where((row_flags == 1)[:, None], placed, jnp.zeros_like(placed))
    return (
        placed[:, :feature_width][None],
        placed[:, feature_width : 2 * feature_width][None],
        placed[:, 2 * feature_width :][None],
        grad_weight,
    )


def solution(mesh):
    in_specs = (
        P("dp", "seq", None),
        P("dp", "seq", None),
        P("dp", "seq", None),
        P("dp", "seq", None),
        P(),
        P("dp", "seq"),
    )
    out_specs = (P("dp", "seq", None), P("dp", "seq", None), P("dp", "seq", None), P("seq", None))
    return jax.shard_map(
        per_device, mesh=mesh, in_specs=in_specs, out_specs=out_specs, check_vma=False
    )
```

profile of v0, /device:TPU:17, one launch (start us, length us, event | category | flops | bytes accessed | tf_op | source)
XLA Modules:
  0.0 647.4 jit_solution(8209230128436905229)
XLA Ops:
  13.7 3.2 pad_maximum_fusion
  16.9 4.5 gather_fusion
  30.0 118.5 %all-reduce = bf16[4608]{0:T(1024)(128)(2,1)S(1)} all-reduce(bf16[4608]{0:T(1024)(128)(2,1)S(1)} %dynamic-update-slice), channel_id=1, replica_groups=mesh['dp'=8,'seq'=32] {'seq'}, use_global_device_ids=true, to_apply=%add | all-reduce | flops 4608 | bytes 18432
  150.0 8.9 %copy.58 = bf16[4608,640]{0,1:T(8,128)(2,1)} copy(bf16[4608,640]{1,0:T(8,128)(2,1)} %all-gather.7.cloned.1.call-done) | data formatting | bytes 11796480 | tf_op jit(solution)/shard_map/all_gather | solution.py:48
  158.9 38.9 %all-gather.9.cloned.1.call-done = bf16[4608,640]{1,0:T(8,128)(2,1)} async-done(((bf16[144,640]{1,0:T(8,128)(2,1)}), bf16[4608,640]{1,0:T(8,128)(2,1)}) %all-gather.9.cloned.1.call-update) | async-done | bytes 5898256 | tf_op jit(solution)/shard_map/all_gather | solution.py:49
  197.9 8.9 %copy.59 = bf16[4608,640]{0,1:T(8,128)(2,1)} copy(bf16[4608,640]{1,0:T(8,128)(2,1)} %all-gather.9.cloned.1.call-done) | data formatting | bytes 11796480 | tf_op jit(solution)/shard_map/all_gather | solution.py:49
  206.7 61.8 %while.29 = (s32[]{:T(128)}, bf16[8,144,80]{2,1,0:T(8,128)(2,1)}, bf16[8,144,80]{2,1,0:T(8,128)(2,1)}, f32[8,144]{1,0:T(8,128)S(1)}, f32[8,144]{1,0:T(8,128)S(1)...) while((s32[]{:T(128)}, bf16[8,144,80]{2,1,0:T(8,128)(2,1)}, ...), condition=%wide.region_8.9_spmd, body=%wide.region_4.8_spmd.sunk | while | flops 432704736 | bytes 13800833 | solution.py:82
  211.4 3.0 fusion.110
  219.2 2.9 fusion.110
  226.9 2.9 fusion.110
  234.6 2.9 fusion.110
  242.3 2.9 fusion.110
  250.0 2.9 fusion.110
  257.7 2.9 fusion.110
  265.4 3.0 fusion.110
  268.5 38.2 %all-gather = f32[32,144,8]{1,2,0:T(8,128)S(1)} all-gather(f32[1,144,8]{1,2,0:T(8,128)S(1)} %bitcast.195), channel_id=1, replica_groups=mesh['dp'=8,'seq'=32] {'seq'}, dimensions={0}, use_global_device_ids=true | all-gather | bytes 152064 | tf_op jit(solution)/shard_map/all_gather | solution.py:92
  306.9 36.6 %all-gather.1 = f32[32,144,8]{1,2,0:T(8,128)S(1)} all-gather(f32[1,144,8]{1,2,0:T(8,128)S(1)} %bitcast.196), channel_id=1, replica_groups=mesh['dp'=8,'seq'=32] {'seq'}, dimensions={0}, use_global_device_ids=true | all-gather | bytes 152064 | tf_op jit(solution)/shard_map/all_gather | solution.py:93
  345.0 3.3 fusion.81
  348.4 9.0 %copy.64 = bf16[4608,640]{0,1:T(8,128)(2,1)} copy(bf16[4608,640]{1,0:T(8,128)(2,1)} %all-gather.11.cloned.1.call-done) | data formatting | bytes 11796480 | tf_op jit(solution)/shard_map/all_gather | solution.py:97
  357.4 14.2 %all-gather.13.cloned.1.call-done = bf16[4608,640]{1,0:T(8,128)(2,1)} async-done(((bf16[144,640]{1,0:T(8,128)(2,1)}), bf16[4608,640]{1,0:T(8,128)(2,1)}) %all-gather.13.cloned.1.call-update) | async-done | bytes 5898256 | tf_op jit(solution)/shard_map/all_gather | solution.py:98
  371.6 8.9 %copy.67 = bf16[4608,640]{0,1:T(8,128)(2,1)} copy(bf16[4608,640]{1,0:T(8,128)(2,1)} %all-gather.13.cloned.1.call-done) | data formatting | bytes 11796480 | tf_op jit(solution)/shard_map/all_gather | solution.py:98
  380.5 56.9 %while.30 = (s32[]{:T(128)}, bf16[8,144,80]{2,1,0:T(8,128)(2,1)S(1)}, bf16[8,144,80]{2,1,0:T(8,128)(2,1)}, bf16[8,4608,80]{1,2,0:T(8,128)(2,1)}, bf16[8,144,80]{...) while((s32[]{:T(128)}, ...), condition=%wide.region_10.11_spmd.clone, body=%wide.region_9.10_spmd.clone.sunk | while | flops 429981824 | bytes 11250069 | solution.py:125
  440.3 3.2 gather_fusion.1
  446.9 192.4 %all-reduce.3.cloned.1.call-done = f32[640,1280]{1,0:T(8,128)} async-done(((f32[640,1280]{1,0:T(8,128)}), f32[640,1280]{1,0:T(8,128)}) %all-reduce.3.cloned.1.call-update) | async-done | bytes 3276816 | tf_op jit(solution)/shard_map/psum | solution.py:141
  (178 shorter events, 120.1 us)
Async XLA Ops:
  7.2 16.9 %copy-start = (bf16[640,1280]{1,0:T(8,128)(2,1)S(1)}, bf16[640,1280]{1,0:T(8,128)(2,1)}, u32[]{:S(2)}) copy-start(bf16[640,1280]{1,0:T(8,128)(2,1)} %param.14) | copy-start | bytes 4915204
  7.2 142.8 %all-gather.7.cloned.1.call-start = ((), (), s32[]{:S(2)}) async-start(), calls=%async_computation | async-start | bytes 6082560 | tf_op jit(solution)/shard_map/all_gather | solution.py:48
  21.6 6.4 copy-start.2
  22.5 3.0 copy-start.3
  22.5 5.2 copy-start.4
  22.5 5.5 copy-start.5
  22.5 5.9 copy-start.7
  22.5 175.3 %all-gather.9.cloned.1.call-start = ((), (), s32[]{:S(2)}) async-start(), calls=%async_computation.1 | async-start | bytes 6082560 | tf_op jit(solution)/shard_map/all_gather | solution.py:49
  23.3 325.1 %all-gather.11.cloned.1.call-start = ((), (), s32[]{:S(2)}) async-start(), calls=%async_computation.2 | async-start | bytes 6082560 | tf_op jit(solution)/shard_map/all_gather | solution.py:97
  24.0 4.5 copy-start.8
  24.0 347.5 %all-gather.13.cloned.1.call-start = ((), (), s32[]{:S(2)}) async-start(), calls=%async_computation.3 | async-start | bytes 6082560 | tf_op jit(solution)/shard_map/all_gather | solution.py:98
  25.4 613.9 %all-reduce.3.cloned.1.call-start = ((), (), s32[]{:S(2)}) async-start(), calls=%async_computation.4 | async-start | bytes 6553600 | tf_op jit(solution)/shard_map/psum | solution.py:141
  357.4 23.1 %copy-start.6 = (bf16[8,144,80]{2,1,0:T(8,128)(2,1)S(1)}, bf16[8,144,80]{2,1,0:T(8,128)(2,1)}, u32[]{:S(2)}) copy-start(bf16[8,144,80]{2,1,0:T(8,128)(2,1)} %custom-call.8) | copy-start | bytes 552964
  443.5 197.4 %copy-start.1 = (bf16[640,1280]{1,0:T(8,128)(2,1)S(1)}, bf16[640,1280]{1,0:T(8,128)(2,1)}, u32[]{:S(2)}) copy-start(bf16[640,1280]{1,0:T(8,128)(2,1)} %param.14) | copy-start | bytes 4915204
Sparse Core Ops, SparseCore 0:
  22.6 88.7 all-gather.6
  114.0 83.7 all-gather.8
  200.5 84.2 all-gather.10
  287.2 84.3 all-gather.12
  376.9 262.3 all-reduce.2
where the time goes:
time: 652 us; the launch traced here: 647 us
  waiting for transfers between devices  247 us (38%)
  blocking collectives  193 us (30%)
  matrix products  112 us (17%)
  local copies, waits for them, and re-layouts  60.3 us (9%)
  other arithmetic  19.7 us (3%)
  between operations  14.8 us (2%)
    psum x1, waiting for transfers between devices, per_device(): weight_whole = lax.psum(weight_term, ('dp', 'seq'))  192 us
    unnamed x1, blocking collectives  118 us
    all_gather x1, waiting for transfers between devices, per_device(): lax.all_gather(value_rows, 'seq', axis=0, tiled=True)  38.9 us
    all_gather x1, blocking collectives, per_device(): lax.all_gather(log_total, 'seq', axis=1, tiled=True)  38.2 us
    all_gather x1, blocking collectives, per_device(): lax.all_gather(row_delta, 'seq', axis=1, tiled=True)  36.6 us
    dot_general x8, matrix products, own_rows(): jnp.dot(grad_score, key_head, preferred_element_type=jnp.float32)  23.5 us
    dot_general x8, matrix products, one_head(): lax.dot_general(grad_score, query_head, (((0,), (0,)), ((), ())), preferr...  18.7 us
    dot_general x8, matrix products, own_rows(): jnp.dot(weights, value_head, preferred_element_type=jnp.float32)  18.4 us
  transfers between devices with their start and end apart: 5, of which 3 were waited for; matrix products, arithmetic and copies ran while one was open for 27% of the time, Pallas kernels for 0%

commit v1 on v0

v1 whole, which is shorter than its diff:
```python
import functools

import jax
import jax.numpy as jnp
from jax import lax
from jax.experimental import pallas as pl
from jax.experimental.pallas import tpu as pltpu
from jax.sharding import PartitionSpec as P

HEAD_DIM = 80
VIS_MAX = 144
Z_RING = 8
Y_RING = 4

BF16 = jnp.bfloat16
F32 = jnp.float32
MESH = pl.DeviceIdType.MESH
FAR = 1e30


def nn(a, b):
    return jnp.dot(a, b, preferred_element_type=F32)


def nt(a, b):
    return lax.dot_general(a, b, (((1,), (1,)), ((), ())), preferred_element_type=F32)


def identity(n):
    rows = lax.broadcasted_iota(jnp.int32, (n, n), 0)
    cols = lax.broadcasted_iota(jnp.int32, (n, n), 1)
    return jnp.where(rows == cols, 1.0, 0.0).astype(BF16)


def lane_iota(rows, lanes):
    return lax.broadcasted_iota(jnp.int32, (rows, lanes), 1)


class Sizes:
    def __init__(self, nx, nz, ny, rows, cap, heads, width):
        self.nx, self.nz, self.ny = nx, nz, ny
        self.rows, self.cap, self.heads, self.width = rows, cap, heads, width
        self.pairs = nz // 2
        self.queries = self.pairs * cap
        self.keys = nx * self.queries
        self.block = 256 if self.keys % 256 == 0 else 128
        self.hd = heads * HEAD_DIM
        self.col_tiles = width // 128
        self.tiles = (HEAD_DIM // 16) * self.col_tiles
        self.share = -(-self.tiles // nz)
        self.out_rows = self.hd // (nx * nz)
        self.per_head = HEAD_DIM // self.out_rows


def kernel(
    sz,
    vis_ref, q_hbm, k_hbm, v_hbm, u_hbm, w_hbm,
    gq_hbm, gk_hbm, gv_hbm, gw_ref,
    qin, kin, vin, uin, win,
    send_a, recv_a, send_b, recv_b,
    kv, kvt, q_mask, q_zero, d_out, scores,
    send_e, recv_e, dkv, recv_c, send_d, recv_d,
    upk, wown, wsend1, wrecv1, wsend2, wrecv2, red, tiles, wrecv3, wsend4, wrecv4, wsend5, wrecv5,
    full, stage,
    load_sem, store_sem,
    a_s, a_r, b_s, b_r, g_s, g_r, e_s, e_r, c_s, c_r, d_s, d_r,
    w1_s, w1_r, w2_s, w2_r, w3_s, w3_r, w4_s, w4_r, w5_s, w5_r, w6_s, w6_r,
):
    nx, nz, ny, cap, heads = sz.nx, sz.nz, sz.ny, sz.cap, sz.heads
    nq, nk, blk, width = sz.queries, sz.keys, sz.block, sz.width
    scale = HEAD_DIM ** -0.5
    dp = lax.axis_index("dp")
    seq = lax.axis_index("seq")
    x, z = lax.div(seq, nz), lax.rem(seq, nz)
    y, core = lax.div(dp, 2), lax.rem(dp, 2)

    def z_peer(k):
        return lax.rem(z + k, nz)

    def x_peer(k):
        return lax.rem(x + k, nx)

    def at_z(k):
        return (dp, x * nz + z_peer(k))

    def at_x(k):
        return (dp, x_peer(k) * nz + z)

    def at_y(k):
        return (lax.rem(y + k, ny) * 2 + core, seq)

    def remote(src, dst, ss, rs, dev):
        return pltpu.make_async_remote_copy(
            src_ref=src, dst_ref=dst, send_sem=ss, recv_sem=rs, device_id=dev, device_id_type=MESH
        )

    barrier = pltpu.get_barrier_semaphore()
    peers = [at_z(k) for k in range(1, nz)] + [at_x(k) for k in range(1, nx)]
    peers += [(lax.rem(dp + k, 2 * ny), seq) for k in range(1, 2 * ny)]
    for peer in peers:
        pl.semaphore_signal(barrier, inc=1, device_id=peer, device_id_type=MESH)

    loads = []
    for i, (src, dst) in enumerate(
        [(v_hbm, vin), (k_hbm, kin), (q_hbm, qin), (u_hbm, uin), (w_hbm, win)]
    ):
        source = src.at[0] if i < 4 else src
        loads.append(pltpu.make_async_copy(source, dst, load_sem.at[i]))
        loads[-1].start()

    seen = vis_ref[...].astype(F32)
    rows = sz.rows
    upto = (
        lax.broadcasted_iota(jnp.int32, (rows, rows), 0)
        <= lax.broadcasted_iota(jnp.int32, (rows, rows), 1)
    )
    count = nn(jnp.broadcast_to(seen, (16, rows)).astype(BF16), jnp.where(upto, 1.0, 0.0).astype(BF16))
    rank = count[0:1, :].astype(jnp.int32) - 1
    odd = lax.rem(z, 2)
    slot = jnp.where(odd == 1, cap - 1 - rank, rank)
    slot = jnp.where(seen > 0.5, slot, -1)
    pick = jnp.where(lax.broadcasted_iota(jnp.int32, (cap, rows), 0) == slot, 1.0, 0.0)
    live = jnp.sum(pick, axis=1, keepdims=True)
    pick = pick.astype(BF16)

    for i in range(3):
        loads[i].wait()
    pv, pk, pq = nn(pick, vin[...]), nn(pick, kin[...]), nn(pick, qin[...])
    for h in range(heads):
        cols = slice(HEAD_DIM * h, HEAD_DIM * (h + 1))
        send_a[h] = jnp.concatenate(
            [pv[:, cols], pk[:, cols], pq[:, cols], jnp.broadcast_to(live, (cap, 16))], axis=1
        ).astype(BF16)

    pl.semaphore_wait(barrier, len(peers))

    def all_z(src, dst, ss, rs, start):
        copies = [remote(src(z_peer(k)), dst, ss.at[k - 1], rs.at[k - 1], at_z(k)) for k in range(1, nz)]
        if start:
            for copy in copies:
                copy.start()
        return copies

    a_copies = all_z(lambda t: send_a.at[t], recv_a.at[z], a_s, a_r, True)

    loads[3].wait()
    upk[...] = nn(pick, uin[...]).astype(BF16)
    loads[4].wait()
    send_b[...] = jnp.zeros_like(send_b)
    for h in range(heads):
        part = nt(upk[...], win[HEAD_DIM * h : HEAD_DIM * (h + 1), :])
        send_b[h, :, 0:HEAD_DIM] = part.astype(BF16)
    b_copies = all_z(lambda t: send_b.at[t], recv_b.at[z], b_s, b_r, True)

    recv_a[z] = send_a[z]
    recv_b[z] = send_b[z]
    eye = identity(256)
    unpick = nt(identity(rows), pick).astype(BF16)

    for copy in a_copies:
        copy.wait()
    flag = jnp.where(lane_iota(1, 256) >= 240, 1.0, 0.0)
    base = pl.multiple_of(x * nq, 16)
    for p in range(sz.pairs):
        both = recv_a[2 * p].astype(F32) + recv_a[2 * p + 1].astype(F32) - flag
        kv[pl.ds(base + p * cap, cap), :] = both.astype(BF16)
    g_copies = [
        remote(kv.at[pl.ds(base, nq)], kv.at[pl.ds(base, nq)], g_s.at[k - 1], g_r.at[k - 1], at_x(k))
        for k in range(1, nx)
    ]
    for copy in g_copies:
        copy.start()
    own = pltpu.roll(kv[pl.ds(base, nq), :].astype(F32), 256 - HEAD_DIM, 1)
    lanes = lane_iota(nq, 256)
    own = jnp.where((lanes >= HEAD_DIM) & (lanes < 2 * HEAD_DIM), own, 0.0)
    q_zero[...] = own.astype(BF16)
    q_mask[...] = jnp.where(lanes == 240, FAR, own).astype(BF16)

    def score_group(at):
        part = kv[pl.ds(at, nq), :]
        scores[pl.ds(at, nq), :] = nt(part, q_mask[...])

    score_group(base)

    for copy in b_copies:
        copy.wait()
    d_out[...] = jnp.zeros_like(d_out)
    for p in range(sz.pairs):
        both = recv_b[2 * p].astype(F32) + recv_b[2 * p + 1].astype(F32)
        d_out[p * cap : (p + 1) * cap, 0:128] = both.astype(BF16)
    d_out_t = nt(eye[0:HEAD_DIM, 0:128], d_out[:, 0:128])

    for k in range(1, nx):
        g_copies[k - 1].wait()
        score_group(pl.multiple_of(lax.rem(x + nx - k, nx) * nq, 16))

    steps = nk // blk

    def at_step(i):
        return pl.ds(pl.multiple_of(i * blk, blk), blk)

    def max_step(i, top):
        return jnp.maximum(top, jnp.max(scores[at_step(i), :], axis=0, keepdims=True))

    top = lax.fori_loop(0, steps, max_step, jnp.full((1, nq), -3e38, F32))

    def exp_step(i, total):
        e = jnp.exp((scores[at_step(i), :] - top) * scale)
        scores[at_step(i), :] = e
        kvt[:, at_step(i)] = nt(eye, kv[at_step(i), :]).astype(BF16)
        return total + jnp.sum(e, axis=0, keepdims=True)

    total = lax.fori_loop(0, steps, exp_step, jnp.zeros((1, nq), F32))
    inverse = 1.0 / total

    def attend_step(i, acc):
        w = (scores[at_step(i), :] * inverse).astype(BF16)
        return acc + nn(kvt[0:HEAD_DIM, at_step(i)], w)

    attended_t = lax.fori_loop(0, steps, attend_step, jnp.zeros((HEAD_DIM, nq), F32)).astype(BF16)
    eye_q = identity(nq)
    send_e[...] = jnp.zeros_like(send_e)
    attended = nt(eye_q, attended_t).astype(BF16)
    for p in range(sz.pairs):
        send_e[p, :, 0:HEAD_DIM] = attended[p * cap : (p + 1) * cap, :]
    e_copies = all_z(lambda t: send_e.at[lax.div(t, 2)], recv_e.at[z], e_s, e_r, True)
    recv_e[z] = send_e[lax.div(z, 2)]

    delta = jnp.sum(d_out_t * attended_t.astype(F32), axis=0, keepdims=True)
    slope = inverse * scale

    def back_step(i, acc):
        e = scores[at_step(i), :]
        w = (e * inverse).astype(BF16)
        grad_prob = nt(kv[at_step(i), :], d_out[...])
        ds = (e * slope * (grad_prob - delta)).astype(BF16)
        dkv[at_step(i), :] = (nn(ds, q_zero[...]) + nn(w, d_out[...])).astype(BF16)
        return acc + nn(kvt[HEAD_DIM : 2 * HEAD_DIM, at_step(i)], ds)

    dq_t = lax.fori_loop(0, steps, back_step, jnp.zeros((HEAD_DIM, nq), F32)).astype(BF16)

    c_copies = [
        remote(
            dkv.at[pl.ds(pl.multiple_of(x_peer(k) * nq, 16), nq)],
            recv_c.at[k - 1], c_s.at[k - 1], c_r.at[k - 1], at_x(k),
        )
        for k in range(1, nx)
    ]
    for copy in c_copies:
        copy.start()

    for copy in e_copies:
        copy.wait()
    half = heads // 2

    def weight_term(h):
        att = nt(eye[0:128, 0:128], recv_e[h])[0:HEAD_DIM, :].astype(BF16)
        return nn(att, upk[...])

    def other_half(i, carry):
        wsend1[i] = weight_term((1 - core) * half + i).astype(BF16)
        return carry

    lax.fori_loop(0, half, other_half, 0)
    w1 = remote(wsend1, wrecv1, w1_s, w1_r, (y * 2 + 1 - core, seq))
    w1.start()

    def own_half(i, carry):
        wown[i] = weight_term(core * half + i)
        return carry

    lax.fori_loop(0, half, own_half, 0)

    dq = nt(eye_q, dq_t)
    dq = jnp.concatenate(
        [jnp.zeros((nq, 2 * HEAD_DIM), F32), dq, jnp.zeros((nq, 16), F32)], axis=1
    )

    w1.wait()

    def join_half(i, carry):
        wown[i] = wown[i] + wrecv1[i].astype(F32)
        wsend2[i] = wown[i].astype(BF16)
        return carry

    lax.fori_loop(0, half, join_half, 0)
    w2 = [
        remote(
            wsend2.at[lax.rem(y + k, ny)], wrecv2.at[k - 1], w2_s.at[k - 1], w2_r.at[k - 1], at_y(k)
        )
        for k in range(1, ny)
    ]
    for copy in w2:
        copy.start()

    for copy in c_copies:
        copy.wait()
    mine = dkv[pl.ds(base, nq), :].astype(F32) + dq
    for k in range(1, nx):
        mine = mine + recv_c[k - 1].astype(F32)
    mine = mine.astype(BF16)
    for p in range(sz.pairs):
        send_d[p] = mine[p * cap : (p + 1) * cap, :]
    d_copies = all_z(lambda t: send_d.at[lax.div(t, 2)], recv_d.at[z], d_s, d_r, True)
    recv_d[z] = send_d[lax.div(z, 2)]

    for copy in w2:
        copy.wait()
    red[...] = wown[y]
    for k in range(1, ny):
        red[...] = red[...] + wrecv2[k - 1].astype(F32)
    tiles[...] = jnp.zeros_like(tiles)
    for r in range(HEAD_DIM // 16):
        for c in range(sz.col_tiles):
            tiles[r * sz.col_tiles + c] = red[16 * r : 16 * r + 16, 128 * c : 128 * c + 128].astype(BF16)
    share = sz.share
    w3 = [
        remote(
            tiles.at[pl.ds(z_peer(k) * share, share)],
            wrecv3.at[k - 1], w3_s.at[k - 1], w3_r.at[k - 1], at_z(k),
        )
        for k in range(1, nz)
    ]
    for copy in w3:
        copy.start()

    for copy in d_copies:
        copy.wait()
    stores = []
    for t, dst in enumerate((gv_hbm, gk_hbm, gq_hbm)):
        at = t * HEAD_DIM
        merged = jnp.concatenate(
            [recv_d[h].astype(F32)[:, at : at + HEAD_DIM] for h in range(heads)], axis=1
        ).astype(BF16)
        stage[t] = nn(unpick, merged).astype(BF16)
        stores.append(pltpu.make_async_copy(stage.at[t], dst.at[0], store_sem.at[t]))
        stores[-1].start()

    for copy in w3:
        copy.wait()
    part = tiles[pl.ds(z * share, share)].astype(F32)
    for k in range(1, nz):
        part = part + wrecv3[k - 1].astype(F32)
    wsend4[...] = part
    w4 = [
        remote(wsend4, wrecv4.at[k - 1], w4_s.at[k - 1], w4_r.at[k - 1], at_x(k)) for k in range(1, nx)
    ]
    for copy in w4:
        copy.start()
    for copy in w4:
        copy.wait()
    for k in range(1, nx):
        part = part + wrecv4[k - 1]
    wsend5[...] = part
    w5 = all_z(lambda t: wsend5, wrecv5.at[z], w5_s, w5_r, True)
    wrecv5[z] = wsend5[...]
    for copy in w5:
        copy.wait()
    for r in range(HEAD_DIM // 16):
        for c in range(sz.col_tiles):
            t = r * sz.col_tiles + c
            full[16 * r : 16 * r + 16, 128 * c : 128 * c + 128] = wrecv5[t // share, t % share]

    out_rows, per_head = sz.out_rows, sz.per_head
    head = lax.div(seq, per_head)
    owner = dp == lax.rem(head, half) * 2 + lax.div(head, half)
    w6 = [
        remote(gw_ref, gw_ref, w6_s.at[k - 1], w6_r, (lax.rem(dp + k, 2 * ny), seq))
        for k in range(1, 2 * ny)
    ]

    @pl.when(owner)
    def _():
        for q in range(per_head):

            @pl.when(lax.rem(seq, per_head) == q)
            def _():
                gw_ref[...] = full[out_rows * q : out_rows * (q + 1), :]

        for copy in w6:
            copy.start()
        for copy in w6:
            copy.wait_send()

    @pl.when(jnp.logical_not(owner))
    def _():
        w6[0].wait_recv()

    for copy in stores:
        copy.wait()


def per_device(sz, queries, keys, values, upstream, out_weight, visible):
    nx, nz, ny, cap, heads = sz.nx, sz.nz, sz.ny, sz.cap, sz.heads
    nq, nk, hd, width, rows = sz.queries, sz.keys, sz.hd, sz.width, sz.rows
    half, share = heads // 2, sz.share
    hbm = pl.BlockSpec(memory_space=pl.ANY)
    vmem = pl.BlockSpec(memory_space=pltpu.VMEM)
    grad = jax.ShapeDtypeStruct((1, rows, hd), BF16)
    dma = pltpu.SemaphoreType.DMA
    buffers = [
        ((rows, hd), BF16), ((rows, hd), BF16), ((rows, hd), BF16), ((rows, width), BF16), ((hd, width), BF16),
        ((heads, cap, 256), BF16), ((heads, cap, 256), BF16),
        ((heads, cap, 128), BF16), ((heads, cap, 128), BF16),
        ((nk, 256), BF16), ((256, nk), BF16), ((nq, 256), BF16), ((nq, 256), BF16), ((nq, 256), BF16),
        ((nk, nq), F32),
        ((sz.pairs, cap, 128), BF16), ((heads, cap, 128), BF16),
        ((nk, 256), BF16), ((nx - 1, nq, 256), BF16),
        ((sz.pairs, cap, 256), BF16), ((heads, cap, 256), BF16),
        ((cap, width), BF16),
        ((half, HEAD_DIM, width), F32), ((half, HEAD_DIM, width), BF16), ((half, HEAD_DIM, width), BF16),
        ((half, HEAD_DIM, width), BF16), ((ny - 1, HEAD_DIM, width), BF16),
        ((HEAD_DIM, width), F32),
        ((share * nz, 16, 128), BF16), ((nz - 1, share, 16, 128), BF16),
        ((share, 16, 128), F32), ((nx - 1, share, 16, 128), F32),
        ((share, 16, 128), F32), ((nz, share, 16, 128), F32),
        ((HEAD_DIM, width), F32), ((3, rows, hd), BF16),
    ]
    zs, xs, ys, one = dma((nz - 1,)), dma((nx - 1,)), dma((ny - 1,)), dma
    scratch = [pltpu.VMEM(shape, kind) for shape, kind in buffers]
    scratch += [dma((5,)), dma((3,))]
    scratch += [zs, zs, zs, zs, xs, xs, zs, zs, xs, xs, zs, zs]
    scratch += [one, one, ys, ys, zs, zs, xs, xs, zs, zs, dma((2 * ny - 1,)), one]
    return pl.pallas_call(
        functools.partial(kernel, sz),
        out_shape=(grad, grad, grad, jax.ShapeDtypeStruct((sz.out_rows, width), F32)),
        in_specs=[vmem] + [hbm] * 5,
        out_specs=(hbm, hbm, hbm, vmem),
        scratch_shapes=scratch,
        compiler_params=pltpu.CompilerParams(
            collective_id=0, has_side_effects=True, vmem_limit_bytes=56 * 1024 * 1024
        ),
    )(visible, queries, keys, values, upstream, out_weight)


def build(mesh, nz, ny, cap):
    n_seq = mesh.shape["seq"]

    def run(queries, keys, values, upstream, out_weight, visible):
        hd, width = out_weight.shape
        sz = Sizes(n_seq // nz, nz, ny, queries.shape[1], cap, hd // HEAD_DIM, width)
        return per_device(sz, queries, keys, values, upstream, out_weight, visible)

    part = P("dp", "seq", None)
    return jax.shard_map(
        run,
        mesh=mesh,
        in_specs=(part, part, part, part, P(), P("dp", "seq")),
        out_specs=(part, part, part, P("seq", None)),
        check_vma=False,
    )


def solution(mesh):
    return build(mesh, Z_RING, Y_RING, VIS_MAX)
```

time: 652 us -> 113 us (0.17)
  waiting for transfers between devices: 247 us -> 0 us
  blocking collectives: 193 us -> 0 us
  matrix products: 112 us -> 0 us
  Pallas kernels: 0 us -> 108 us
  local copies, waits for them, and re-layouts: 60.3 us -> 4.41 us
  other arithmetic: 19.7 us -> 0 us
  between operations: 14.8 us -> 0.66 us
    psum x1 -> x0, waiting for transfers between devices: 192 us -> none  [per_device(): weight_whole = lax.psum(weight_term, ('dp', 'seq'))]
    unnamed x1 -> x0, blocking collectives: 118 us -> none
    dot_general x50 -> x0, matrix products: 112 us -> none  [the longest x8 23.5 us: own_rows(): jnp.dot(grad_score, key_head, preferred_element_type=jnp.float32)]
    pallas_call x0 -> x1, Pallas kernels: none -> 108 us  [per_device(): pl.pallas_call(functools.partial(kernel, sz), out_shape=(grad, grad, grad...]
    all_gather x2 -> x0, blocking collectives: 74.7 us -> none  [the longest x1 38.2 us: per_device(): lax.all_gather(log_total, 'seq', axis=1, tiled=True)]
    all_gather x4 -> x0, waiting for transfers between devices: 53.2 us -> none  [the longest x1 38.9 us: per_device(): lax.all_gather(value_rows, 'seq', axis=0, tiled=True)]
    all_gather x6 -> x0, local copies, waits for them, and re-layouts: 35.9 us -> none  [the longest x1 8.99 us: per_device(): query_piece = lax.all_gather(query_rows, 'seq', axis=0, tiled=True)]
    gather x2 -> x0, local copies, waits for them, and re-layouts: 7.68 us -> none  [the longest x1 4.46 us: per_device(): taken = jnp.take(payload, source_rows, axis=0)]
  transfers between devices with their start and end apart: 5 -> 0, of which waited for: 3 -> 0; matrix products, arithmetic and copies ran while one was open for 27% -> 0% of each run, Pallas kernels for 0% -> 0%
where the time goes in v1:
time: 113 us
  Pallas kernels  108 us (96%)
  local copies, waits for them, and re-layouts  4.41 us (4%)
    pallas_call x1, Pallas kernels, per_device(): pl.pallas_call(functools.partial(kernel, sz), out_shape=(grad, grad, grad...  108 us
    unnamed x10, local copies, waits for them, and re-layouts  4.41 us

profile of v1, /device:TPU:17, one launch (start us, length us, event | category | flops | bytes accessed | tf_op | source)
XLA Modules:
  0.0 112.9 jit_solution(4714815557835905694)
XLA Ops:
  0.6 107.8 %shard_map.93 = (bf16[1,512,640]{2,1,0:T(8,128)(2,1)}, bf16[1,512,640]{2,1,0:T(8,128)(2,1)}, bf16[1,512,640]{2,1,0:T(8,128)(2,1)}, f32[20,1280]{1,0:T(8,128)}) custom-call(s32[1,512]{1,0:T(1,128)} %vis_ref.1, bf16[1,512,640]{2,1,0:T(8,128)(2,1)} %q_hbm.1, bf16[1,512,640]{2,1,0:T(8,128)(2,1)} %k_hbm.1, bf16[1,512,640]{2,1,0:T(8,128)(2,1)} %v_hbm.1, ...), custom_call_target="tpu_custom_call" | custom-call | tf_op jit(solution)/shard_map/pallas_call | solution.py:424
  108.5 0.0 copy-start.1
  108.5 0.0 copy-start
  108.5 2.1 %copy.14 = bf16[1,512,640]{2,1,0:T(8,128)(2,1)} copy(bf16[1,512,640]{2,1,0:T(8,128)(2,1)} %get-tuple-element.8) | data formatting | bytes 1310720
  110.6 0.0 copy-done.1
  110.6 0.0 copy-start.2
  110.6 0.8 copy.15
  111.4 0.0 copy-done
  111.4 0.8 copy.16
  112.2 0.0 copy-done.2
  112.3 0.6 copy.17
Async XLA Ops:
  108.5 2.1 %copy-start.1 = (bf16[1,512,640]{2,1,0:T(8,128)(2,1)S(1)}, bf16[1,512,640]{2,1,0:T(8,128)(2,1)}, u32[]{:S(2)}) copy-start(bf16[1,512,640]{2,1,0:T(8,128)(2,1)} %get-tuple-element.9) | copy-start | bytes 1966084
  108.5 2.9 %copy-start = (bf16[1,512,640]{2,1,0:T(8,128)(2,1)S(1)}, bf16[1,512,640]{2,1,0:T(8,128)(2,1)}, u32[]{:S(2)}) copy-start(bf16[1,512,640]{2,1,0:T(8,128)(2,1)} %get-tuple-element.10) | copy-start | bytes 1966084
  110.6 1.7 %copy-start.2 = (f32[20,1280]{1,0:T(8,128)S(1)}, f32[20,1280]{1,0:T(8,128)}, u32[]{:S(2)}) copy-start(f32[20,1280]{1,0:T(8,128)} %get-tuple-element.11) | copy-start | bytes 307204

commit v2 on v1

--- a/solution.py
+++ b/solution.py
@@ -43,11 +43,11 @@
         self.pairs = nz // 2
         self.queries = self.pairs * cap
         self.keys = nx * self.queries
-        self.block = 256 if self.keys % 256 == 0 else 128
         self.hd = heads * HEAD_DIM
-        self.col_tiles = width // 128
+        self.half = width // 2
+        self.col_tiles = self.half // 128
         self.tiles = (HEAD_DIM // 16) * self.col_tiles
-        self.share = -(-self.tiles // nz)
+        self.share = -(-self.tiles // self.pairs)
         self.out_rows = self.hd // (nx * nz)
         self.per_head = HEAD_DIM // self.out_rows
 
@@ -60,14 +60,14 @@
     send_a, recv_a, send_b, recv_b,
     kv, kvt, q_mask, q_zero, d_out, scores,
     send_e, recv_e, dkv, recv_c, send_d, recv_d,
-    upk, wown, wsend1, wrecv1, wsend2, wrecv2, red, tiles, wrecv3, wsend4, wrecv4, wsend5, wrecv5,
+    upk, upair, wown, wsend1, wrecv1, wsend2, wrecv2, red, tiles, wrecv3, wsend4, wrecv4, wsend5, wrecv5,
     full, stage,
-    load_sem, store_sem,
+    load_sem, store_sem, u_s, u_r,
     a_s, a_r, b_s, b_r, g_s, g_r, e_s, e_r, c_s, c_r, d_s, d_r,
     w1_s, w1_r, w2_s, w2_r, w3_s, w3_r, w4_s, w4_r, w5_s, w5_r, w6_s, w6_r,
 ):
     nx, nz, ny, cap, heads = sz.nx, sz.nz, sz.ny, sz.cap, sz.heads
-    nq, nk, blk, width = sz.queries, sz.keys, sz.block, sz.width
+    nq, half = sz.queries, sz.half
     scale = HEAD_DIM ** -0.5
     dp = lax.axis_index("dp")
     seq = lax.axis_index("seq")
@@ -150,7 +150,6 @@
     for h in range(heads):
         part = nt(upk[...], win[HEAD_DIM * h : HEAD_DIM * (h + 1), :])
         send_b[h, :, 0:HEAD_DIM] = part.astype(BF16)
-    b_copies = all_z(lambda t: send_b.at[t], recv_b.at[z], b_s, b_r, True)
 
     recv_a[z] = send_a[z]
     recv_b[z] = send_b[z]
@@ -170,17 +169,28 @@
     ]
     for copy in g_copies:
         copy.start()
+    b_copies = all_z(lambda t: send_b.at[t], recv_b.at[z], b_s, b_r, True)
+    u_copy = remote(upk, upair, u_s, u_r, (dp, x * nz + lax.div(z, 2) * 2 + 1 - odd))
+    u_copy.start()
     own = pltpu.roll(kv[pl.ds(base, nq), :].astype(F32), 256 - HEAD_DIM, 1)
     lanes = lane_iota(nq, 256)
     own = jnp.where((lanes >= HEAD_DIM) & (lanes < 2 * HEAD_DIM), own, 0.0)
     q_zero[...] = own.astype(BF16)
     q_mask[...] = jnp.where(lanes == 240, FAR, own).astype(BF16)
 
-    def score_group(at):
-        part = kv[pl.ds(at, nq), :]
-        scores[pl.ds(at, nq), :] = nt(part, q_mask[...])
-
-    score_group(base)
+    def group(k):
+        g = lax.rem(x + nx - k, nx)
+        return g, pl.ds(pl.multiple_of(g * nq, 16), nq)
+
+    def score_group(k, top):
+        g, at = group(k)
+        part = kv[at, :]
+        value = nt(part, q_mask[...])
+        scores[at, :] = value
+        kvt[g] = nt(eye, part).astype(BF16)
+        return jnp.maximum(top, jnp.max(value, axis=0, keepdims=True))
+
+    top = score_group(0, jnp.full((1, nq), -3e38, F32))
 
     for copy in b_copies:
         copy.wait()
@@ -192,84 +202,91 @@
 
     for k in range(1, nx):
         g_copies[k - 1].wait()
-        score_group(pl.multiple_of(lax.rem(x + nx - k, nx) * nq, 16))
-
-    steps = nk // blk
-
-    def at_step(i):
-        return pl.ds(pl.multiple_of(i * blk, blk), blk)
-
-    def max_step(i, top):
-        return jnp.maximum(top, jnp.max(scores[at_step(i), :], axis=0, keepdims=True))
-
-    top = lax.fori_loop(0, steps, max_step, jnp.full((1, nq), -3e38, F32))
-
-    def exp_step(i, total):
-        e = jnp.exp((scores[at_step(i), :] - top) * scale)
-        scores[at_step(i), :] = e
-        kvt[:, at_step(i)] = nt(eye, kv[at_step(i), :]).astype(BF16)
-        return total + jnp.sum(e, axis=0, keepdims=True)
-
-    total = lax.fori_loop(0, steps, exp_step, jnp.zeros((1, nq), F32))
+        top = score_group(k, top)
+
+    total = jnp.zeros((1, nq), F32)
+    for k in range(nx):
+        _, at = group(k)
+        e = jnp.exp((scores[at, :] - top) * scale)
+        scores[at, :] = e
+        total = total + jnp.sum(e, axis=0, keepdims=True)
     inverse = 1.0 / total
 
-    def attend_step(i, acc):
-        w = (scores[at_step(i), :] * inverse).astype(BF16)
-        return acc + nn(kvt[0:HEAD_DIM, at_step(i)], w)
-
-    attended_t = lax.fori_loop(0, steps, attend_step, jnp.zeros((HEAD_DIM, nq), F32)).astype(BF16)
+    attended_t = jnp.zeros((HEAD_DIM, nq), F32)
+    for k in range(nx):
+        g, at = group(k)
+        w = (scores[at, :] * inverse).astype(BF16)
+        attended_t = attended_t + nn(kvt[g, 0:HEAD_DIM, :], w)
+    attended_t = attended_t.astype(BF16)
     eye_q = identity(nq)
     send_e[...] = jnp.zeros_like(send_e)
     attended = nt(eye_q, attended_t).astype(BF16)
     for p in range(sz.pairs):
         send_e[p, :, 0:HEAD_DIM] = attended[p * cap : (p + 1) * cap, :]
-    e_copies = all_z(lambda t: send_e.at[lax.div(t, 2)], recv_e.at[z], e_s, e_r, True)
-    recv_e[z] = send_e[lax.div(z, 2)]
+
+    side = lax.div(z, ny)
+    e_copies = []
+    for p in range(sz.pairs):
+        target = 2 * p + side
+        copy = remote(
+            send_e.at[p], recv_e.at[lax.rem(z, ny)], e_s.at[p], e_r.at[lax.rem(z, ny)], (dp, x * nz + target)
+        )
+        e_copies.append((copy, target != z))
+
+        @pl.when(target != z)
+        def _():
+            copy.start()
+
+        @pl.when(target == z)
+        def _():
+            recv_e[lax.rem(z, ny)] = send_e[p]
 
     delta = jnp.sum(d_out_t * attended_t.astype(F32), axis=0, keepdims=True)
     slope = inverse * scale
 
-    def back_step(i, acc):
-        e = scores[at_step(i), :]
+    dq_t = jnp.zeros((HEAD_DIM, nq), F32)
+    c_copies = []
+    for k in list(range(1, nx)) + [0]:
+        g, at = group(k)
+        e = scores[at, :]
         w = (e * inverse).astype(BF16)
-        grad_prob = nt(kv[at_step(i), :], d_out[...])
+        grad_prob = nt(kv[at, :], d_out[...])
         ds = (e * slope * (grad_prob - delta)).astype(BF16)
-        dkv[at_step(i), :] = (nn(ds, q_zero[...]) + nn(w, d_out[...])).astype(BF16)
-        return acc + nn(kvt[HEAD_DIM : 2 * HEAD_DIM, at_step(i)], ds)
-
-    dq_t = lax.fori_loop(0, steps, back_step, jnp.zeros((HEAD_DIM, nq), F32)).astype(BF16)
-
-    c_copies = [
-        remote(
-            dkv.at[pl.ds(pl.multiple_of(x_peer(k) * nq, 16), nq)],
-            recv_c.at[k - 1], c_s.at[k - 1], c_r.at[k - 1], at_x(k),
-        )
-        for k in range(1, nx)
-    ]
-    for copy in c_copies:
-        copy.start()
-
-    for copy in e_copies:
-        copy.wait()
-    half = heads // 2
-
-    def weight_term(h):
-        att = nt(eye[0:128, 0:128], recv_e[h])[0:HEAD_DIM, :].astype(BF16)
-        return nn(att, upk[...])
-
-    def other_half(i, carry):
-        wsend1[i] = weight_term((1 - core) * half + i).astype(BF16)
-        return carry
-
-    lax.fori_loop(0, half, other_half, 0)
+        dkv[at, :] = (nn(ds, q_zero[...]) + nn(w, d_out[...])).astype(BF16)
+        if k:
+            copy = remote(
+                dkv.at[at], recv_c.at[k - 1], c_s.at[k - 1], c_r.at[k - 1], (dp, g * nz + z)
+            )
+            copy.start()
+            c_copies.append(copy)
+        dq_t = dq_t + nn(kvt[g, HEAD_DIM : 2 * HEAD_DIM, :], ds)
+    dq_t = dq_t.astype(BF16)
+
+    u_copy.wait()
+    upk_all = (upk[...].astype(F32) + upair[...].astype(F32)).astype(BF16)
+    upair[...] = upk_all
+    for i in range(ny):
+        source = odd * ny + i
+
+        @pl.when(source != z)
+        def _():
+            remote(send_e.at[0], recv_e.at[i], e_s.at[0], e_r.at[i], (dp, x * nz + source)).wait_recv()
+
+    for copy, away in e_copies:
+
+        @pl.when(away)
+        def _():
+            copy.wait_send()
+
+    terms = [nt(eye[0:128, 0:128], recv_e[i])[0:HEAD_DIM, :].astype(BF16) for i in range(ny)]
+    other_cols = pl.ds(pl.multiple_of((1 - core) * half, 128), half)
+    own_cols = pl.ds(pl.multiple_of(core * half, 128), half)
+    for i in range(ny):
+        wsend1[i] = nn(terms[i], upair[:, other_cols]).astype(BF16)
     w1 = remote(wsend1, wrecv1, w1_s, w1_r, (y * 2 + 1 - core, seq))
     w1.start()
-
-    def own_half(i, carry):
-        wown[i] = weight_term(core * half + i)
-        return carry
-
-    lax.fori_loop(0, half, own_half, 0)
+    for i in range(ny):
+        wown[i] = nn(terms[i], upair[:, own_cols])
 
     dq = nt(eye_q, dq_t)
     dq = jnp.concatenate(
@@ -278,12 +295,9 @@
 
     w1.wait()
 
-    def join_half(i, carry):
+    for i in range(ny):
         wown[i] = wown[i] + wrecv1[i].astype(F32)
         wsend2[i] = wown[i].astype(BF16)
-        return carry
-
-    lax.fori_loop(0, half, join_half, 0)
     w2 = [
         remote(
             wsend2.at[lax.rem(y + k, ny)], wrecv2.at[k - 1], w2_s.at[k - 1], w2_r.at[k - 1], at_y(k)
@@ -316,10 +330,10 @@
     share = sz.share
     w3 = [
         remote(
-            tiles.at[pl.ds(z_peer(k) * share, share)],
-            wrecv3.at[k - 1], w3_s.at[k - 1], w3_r.at[k - 1], at_z(k),
+            tiles.at[pl.ds(lax.div(z_peer(2 * k), 2) * share, share)],
+            wrecv3.at[k - 1], w3_s.at[k - 1], w3_r.at[k - 1], at_z(2 * k),
         )
-        for k in range(1, nz)
+        for k in range(1, sz.pairs)
     ]
     for copy in w3:
         copy.start()
@@ -338,54 +352,111 @@
 
     for copy in w3:
         copy.wait()
-    part = tiles[pl.ds(z * share, share)].astype(F32)
-    for k in range(1, nz):
+    part = tiles[pl.ds(lax.div(z, 2) * share, share)].astype(F32)
+    for k in range(1, sz.pairs):
         part = part + wrecv3[k - 1].astype(F32)
     wsend4[...] = part
+    per_head, out_rows = sz.per_head, sz.out_rows
+    head = odd * ny + y
+    row = lax.div(head * per_head, nz)
     w4 = [
         remote(wsend4, wrecv4.at[k - 1], w4_s.at[k - 1], w4_r.at[k - 1], at_x(k)) for k in range(1, nx)
     ]
-    for copy in w4:
-        copy.start()
-    for copy in w4:
-        copy.wait()
     for k in range(1, nx):
-        part = part + wrecv4[k - 1]
-    wsend5[...] = part
-    w5 = all_z(lambda t: wsend5, wrecv5.at[z], w5_s, w5_r, True)
-    wrecv5[z] = wsend5[...]
-    for copy in w5:
-        copy.wait()
-    for r in range(HEAD_DIM // 16):
-        for c in range(sz.col_tiles):
-            t = r * sz.col_tiles + c
-            full[16 * r : 16 * r + 16, 128 * c : 128 * c + 128] = wrecv5[t // share, t % share]
-
-    out_rows, per_head = sz.out_rows, sz.per_head
-    head = lax.div(seq, per_head)
-    owner = dp == lax.rem(head, half) * 2 + lax.div(head, half)
+
+        @pl.when(x_peer(k) == row)
+        def _():
+            w4[k - 1].start()
+
+    first = lax.rem(head * per_head, nz)
+    w5 = [
+        remote(
+            wsend5, wrecv5.at[lax.div(z, 2)], w5_s.at[q], w5_r.at[lax.div(z, 2)], (dp, x * nz + first + q)
+        )
+        for q in range(per_head)
+    ]
+
+    @pl.when(x == row)
+    def _():
+        for copy in w4:
+            copy.wait_recv()
+        summed = wsend4[...]
+        for k in range(1, nx):
+            summed = summed + wrecv4[k - 1]
+        wsend5[...] = summed.astype(BF16)
+        for q in range(per_head):
+
+            @pl.when(first + q != z)
+            def _():
+                w5[q].start()
+
+            @pl.when(first + q == z)
+            def _():
+                wrecv5[lax.div(z, 2)] = wsend5[...]
+
+    block = lax.div(seq, per_head)
+    owner = y == lax.rem(block, ny)
     w6 = [
-        remote(gw_ref, gw_ref, w6_s.at[k - 1], w6_r, (lax.rem(dp + k, 2 * ny), seq))
+        remote(
+            gw_ref.at[:, own_cols], gw_ref.at[:, own_cols], w6_s.at[k - 1], w6_r.at[core],
+            (lax.rem(dp + k, 2 * ny), seq),
+        )
         for k in range(1, 2 * ny)
     ]
+    w6_other = remote(
+        gw_ref.at[:, other_cols], gw_ref.at[:, other_cols], w6_s.at[0], w6_r.at[1 - core],
+        (y * 2 + 1 - core, seq),
+    )
 
     @pl.when(owner)
     def _():
+        for j in range(sz.pairs):
+            source = 2 * j + lax.div(block, ny)
+
+            @pl.when(source != z)
+            def _():
+                remote(
+                    wsend5, wrecv5.at[j], w5_s.at[0], w5_r.at[j], (dp, x * nz + source)
+                ).wait_recv()
+
+        for r in range(HEAD_DIM // 16):
+            for c in range(sz.col_tiles):
+                t = r * sz.col_tiles + c
+                full[16 * r : 16 * r + 16, 128 * c : 128 * c + 128] = wrecv5[t // share, t % share].astype(F32)
         for q in range(per_head):
 
             @pl.when(lax.rem(seq, per_head) == q)
             def _():
-                gw_ref[...] = full[out_rows * q : out_rows * (q + 1), :]
+                gw_ref[:, own_cols] = full[out_rows * q : out_rows * (q + 1), :]
 
         for copy in w6:
             copy.start()
-        for copy in w6:
-            copy.wait_send()
 
     @pl.when(jnp.logical_not(owner))
     def _():
         w6[0].wait_recv()
 
+    w6_other.wait_recv()
+
+    @pl.when(owner)
+    def _():
+        for copy in w6:
+            copy.wait_send()
+
+    @pl.when(x == row)
+    def _():
+        for q in range(per_head):
+
+            @pl.when(first + q != z)
+            def _():
+                w5[q].wait_send()
+
+    for k in range(1, nx):
+
+        @pl.when(x_peer(k) == row)
+        def _():
+            w4[k - 1].wait_send()
+
     for copy in stores:
         copy.wait()
 
@@ -393,7 +464,7 @@
 def per_device(sz, queries, keys, values, upstream, out_weight, visible):
     nx, nz, ny, cap, heads = sz.nx, sz.nz, sz.ny, sz.cap, sz.heads
     nq, nk, hd, width, rows = sz.queries, sz.keys, sz.hd, sz.width, sz.rows
-    half, share = heads // 2, sz.share
+    half, share, pairs = sz.half, sz.share, sz.pairs
     hbm = pl.BlockSpec(memory_space=pl.ANY)
     vmem = pl.BlockSpec(memory_space=pltpu.VMEM)
     grad = jax.ShapeDtypeStruct((1, rows, hd), BF16)
@@ -402,25 +473,26 @@
         ((rows, hd), BF16), ((rows, hd), BF16), ((rows, hd), BF16), ((rows, width), BF16), ((hd, width), BF16),
         ((heads, cap, 256), BF16), ((heads, cap, 256), BF16),
         ((heads, cap, 128), BF16), ((heads, cap, 128), BF16),
-        ((nk, 256), BF16), ((256, nk), BF16), ((nq, 256), BF16), ((nq, 256), BF16), ((nq, 256), BF16),
+        ((nk, 256), BF16), ((nx, 256, nq), BF16), ((nq, 256), BF16), ((nq, 256), BF16), ((nq, 256), BF16),
         ((nk, nq), F32),
-        ((sz.pairs, cap, 128), BF16), ((heads, cap, 128), BF16),
+        ((pairs, cap, 128), BF16), ((ny, cap, 128), BF16),
         ((nk, 256), BF16), ((nx - 1, nq, 256), BF16),
         ((sz.pairs, cap, 256), BF16), ((heads, cap, 256), BF16),
-        ((cap, width), BF16),
-        ((half, HEAD_DIM, width), F32), ((half, HEAD_DIM, width), BF16), ((half, HEAD_DIM, width), BF16),
-        ((half, HEAD_DIM, width), BF16), ((ny - 1, HEAD_DIM, width), BF16),
-        ((HEAD_DIM, width), F32),
-        ((share * nz, 16, 128), BF16), ((nz - 1, share, 16, 128), BF16),
+        ((cap, width), BF16), ((cap, width), BF16),
+        ((ny, HEAD_DIM, half), F32), ((ny, HEAD_DIM, half), BF16), ((ny, HEAD_DIM, half), BF16),
+        ((ny, HEAD_DIM, half), BF16), ((ny - 1, HEAD_DIM, half), BF16),
+        ((HEAD_DIM, half), F32),
+        ((share * pairs, 16, 128), BF16), ((pairs - 1, share, 16, 128), BF16),
         ((share, 16, 128), F32), ((nx - 1, share, 16, 128), F32),
-        ((share, 16, 128), F32), ((nz, share, 16, 128), F32),
-        ((HEAD_DIM, width), F32), ((3, rows, hd), BF16),
-    ]
-    zs, xs, ys, one = dma((nz - 1,)), dma((nx - 1,)), dma((ny - 1,)), dma
+        ((share, 16, 128), BF16), ((pairs, share, 16, 128), BF16),
+        ((HEAD_DIM, half), F32), ((3, rows, hd), BF16),
+    ]
+    zs, xs, ys, ps, one = dma((nz - 1,)), dma((nx - 1,)), dma((ny - 1,)), dma((pairs,)), dma
     scratch = [pltpu.VMEM(shape, kind) for shape, kind in buffers]
-    scratch += [dma((5,)), dma((3,))]
-    scratch += [zs, zs, zs, zs, xs, xs, zs, zs, xs, xs, zs, zs]
-    scratch += [one, one, ys, ys, zs, zs, xs, xs, zs, zs, dma((2 * ny - 1,)), one]
+    scratch += [dma((5,)), dma((3,)), one, one]
+    scratch += [zs, zs, zs, zs, xs, xs, ps, dma((ny,)), xs, xs, zs, zs]
+    scratch += [one, one, ys, ys, dma((pairs - 1,)), dma((pairs - 1,)), xs, xs]
+    scratch += [dma((sz.per_head,)), ps, dma((2 * ny - 1,)), dma((2,))]
     return pl.pallas_call(
         functools.partial(kernel, sz),
         out_shape=(grad, grad, grad, jax.ShapeDtypeStruct((sz.out_rows, width), F32)),

time: 113 us -> 101 us (0.89)
  Pallas kernels: 108 us -> 96.1 us
    pallas_call x1, Pallas kernels: 108 us -> 96.1 us  [per_device(): pl.pallas_call(functools.partial(kernel, sz), out_shape=(grad, grad, grad...]
where the time goes in v2:
time: 101 us
  Pallas kernels  96.1 us (95%)
  local copies, waits for them, and re-layouts  4.41 us (4%)
    pallas_call x1, Pallas kernels, per_device(): pl.pallas_call(functools.partial(kernel, sz), out_shape=(grad, grad, grad...  96.1 us
    unnamed x10, local copies, waits for them, and re-layouts  4.41 us

profile of v2, /device:TPU:17, one launch (start us, length us, event | category | flops | bytes accessed | tf_op | source)
XLA Modules:
  0.0 101.2 jit_solution(3025799854087490604)
XLA Ops:
  0.6 96.1 %shard_map.93 = (bf16[1,512,640]{2,1,0:T(8,128)(2,1)}, bf16[1,512,640]{2,1,0:T(8,128)(2,1)}, bf16[1,512,640]{2,1,0:T(8,128)(2,1)}, f32[20,1280]{1,0:T(8,128)}) custom-call(s32[1,512]{1,0:T(1,128)} %vis_ref.1, bf16[1,512,640]{2,1,0:T(8,128)(2,1)} %q_hbm.1, bf16[1,512,640]{2,1,0:T(8,128)(2,1)} %k_hbm.1, bf16[1,512,640]{2,1,0:T(8,128)(2,1)} %v_hbm.1, ...), custom_call_target="tpu_custom_call" | custom-call | tf_op jit(solution)/shard_map/pallas_call | solution.py:496
  96.8 0.0 copy-start.1
  96.8 0.0 copy-start
  96.8 2.1 %copy.14 = bf16[1,512,640]{2,1,0:T(8,128)(2,1)} copy(bf16[1,512,640]{2,1,0:T(8,128)(2,1)} %get-tuple-element.8) | data formatting | bytes 1310720
  98.9 0.0 copy-done.1
  98.9 0.0 copy-start.2
  98.9 0.8 copy.15
  99.7 0.0 copy-done
  99.7 0.8 copy.16
  100.5 0.0 copy-done.2
  100.5 0.6 copy.17
Async XLA Ops:
  96.8 2.1 %copy-start.1 = (bf16[1,512,640]{2,1,0:T(8,128)(2,1)S(1)}, bf16[1,512,640]{2,1,0:T(8,128)(2,1)}, u32[]{:S(2)}) copy-start(bf16[1,512,640]{2,1,0:T(8,128)(2,1)} %get-tuple-element.9) | copy-start | bytes 1966084
  96.8 2.9 %copy-start = (bf16[1,512,640]{2,1,0:T(8,128)(2,1)S(1)}, bf16[1,512,640]{2,1,0:T(8,128)(2,1)}, u32[]{:S(2)}) copy-start(bf16[1,512,640]{2,1,0:T(8,128)(2,1)} %get-tuple-element.10) | copy-start | bytes 1966084
  98.9 1.7 %copy-start.2 = (f32[20,1280]{1,0:T(8,128)S(1)}, f32[20,1280]{1,0:T(8,128)}, u32[]{:S(2)}) copy-start(f32[20,1280]{1,0:T(8,128)} %get-tuple-element.11) | copy-start | bytes 307204

commit v3 on v2

--- a/solution.py
+++ b/solution.py
@@ -16,6 +16,7 @@
 F32 = jnp.float32
 MESH = pl.DeviceIdType.MESH
 FAR = 1e30
+DEAD = 64.0
 
 
 def nn(a, b):
@@ -30,6 +31,16 @@
     rows = lax.broadcasted_iota(jnp.int32, (n, n), 0)
     cols = lax.broadcasted_iota(jnp.int32, (n, n), 1)
     return jnp.where(rows == cols, 1.0, 0.0).astype(BF16)
+
+
+def fold(tail):
+    third = tail.shape[0] // 3
+    parts = [tail[j * third : (j + 1) * third, :] for j in range(3)]
+    return jnp.concatenate(parts + [jnp.zeros((third, 8), F32)], axis=1)
+
+
+def unfold(folded):
+    return jnp.concatenate([folded[:, 40 * j : 40 * j + 40] for j in range(3)], axis=0)
 
 
 def lane_iota(rows, lanes):
@@ -58,11 +69,11 @@
     gq_hbm, gk_hbm, gv_hbm, gw_ref,
     qin, kin, vin, uin, win,
     send_a, recv_a, send_b, recv_b,
-    kv, kvt, q_mask, q_zero, d_out, scores,
-    send_e, recv_e, dkv, recv_c, send_d, recv_d,
+    send_g, recv_g, kv, kvt, q_mask, q_zero, d_out, scores,
+    send_e, recv_e, dkv, send_c, recv_c, send_f, recv_f, send_d, recv_d,
     upk, upair, wown, wsend1, wrecv1, wsend2, wrecv2, red, tiles, wrecv3, wsend4, wrecv4, wsend5, wrecv5,
     full, stage,
-    load_sem, store_sem, u_s, u_r,
+    load_sem, store_sem, u_s, u_r, f_s, f_r,
     a_s, a_r, b_s, b_r, g_s, g_r, e_s, e_r, c_s, c_r, d_s, d_r,
     w1_s, w1_r, w2_s, w2_r, w3_s, w3_r, w4_s, w4_r, w5_s, w5_r, w6_s, w6_r,
 ):
@@ -123,14 +134,20 @@
     live = jnp.sum(pick, axis=1, keepdims=True)
     pick = pick.astype(BF16)
 
-    for i in range(3):
-        loads[i].wait()
-    pv, pk, pq = nn(pick, vin[...]), nn(pick, kin[...]), nn(pick, qin[...])
+    loads[0].wait()
+    loads[1].wait()
+    pv, pk = nn(pick, vin[...]), nn(pick, kin[...])
+    flags = jnp.broadcast_to(live, (cap, 8))
+
+    def put(dst, h, left, right, extra):
+        dst[h, 0:cap, :] = jnp.concatenate([left, right[:, 0:48]], axis=1).astype(BF16)
+        dst[h, cap:, :] = fold(jnp.concatenate([right[:, 48:80], extra], axis=1)).astype(BF16)
+
+    def head_cols(h):
+        return slice(HEAD_DIM * h, HEAD_DIM * (h + 1))
+
     for h in range(heads):
-        cols = slice(HEAD_DIM * h, HEAD_DIM * (h + 1))
-        send_a[h] = jnp.concatenate(
-            [pv[:, cols], pk[:, cols], pq[:, cols], jnp.broadcast_to(live, (cap, 16))], axis=1
-        ).astype(BF16)
+        put(send_a, h, pv[:, head_cols(h)], pk[:, head_cols(h)], flags)
 
     pl.semaphore_wait(barrier, len(peers))
 
@@ -143,13 +160,14 @@
 
     a_copies = all_z(lambda t: send_a.at[t], recv_a.at[z], a_s, a_r, True)
 
+    loads[2].wait()
+    pq = nn(pick, qin[...])
     loads[3].wait()
     upk[...] = nn(pick, uin[...]).astype(BF16)
     loads[4].wait()
-    send_b[...] = jnp.zeros_like(send_b)
     for h in range(heads):
         part = nt(upk[...], win[HEAD_DIM * h : HEAD_DIM * (h + 1), :])
-        send_b[h, :, 0:HEAD_DIM] = part.astype(BF16)
+        put(send_b, h, pq[:, head_cols(h)], part, jnp.zeros((cap, 8), F32))
 
     recv_a[z] = send_a[z]
     recv_b[z] = send_b[z]
@@ -158,25 +176,40 @@
 
     for copy in a_copies:
         copy.wait()
-    flag = jnp.where(lane_iota(1, 256) >= 240, 1.0, 0.0)
     base = pl.multiple_of(x * nq, 16)
+    tails = []
     for p in range(sz.pairs):
-        both = recv_a[2 * p].astype(F32) + recv_a[2 * p + 1].astype(F32) - flag
-        kv[pl.ds(base + p * cap, cap), :] = both.astype(BF16)
+        both = recv_a[2 * p].astype(F32) + recv_a[2 * p + 1].astype(F32)
+        main, rest = both[0:cap, :], unfold(both[cap:, :])
+        dead = rest[:, 32:33] < 0.5
+        tails.append(rest[:, 0:32])
+        mask = jnp.broadcast_to(jnp.where(dead, -1.0, 0.0), (cap, 96))
+        kv[pl.ds(base + p * cap, cap), :] = jnp.concatenate([main, rest[:, 0:32], mask], axis=1).astype(BF16)
+        marked = jnp.where(dead & (lane_iota(cap, 128) == 0), DEAD, main)
+        send_g[p * cap : (p + 1) * cap, :] = marked.astype(BF16)
+    send_g[nq:, 0 : 32 * sz.pairs] = jnp.concatenate(tails, axis=1).astype(BF16)
     g_copies = [
-        remote(kv.at[pl.ds(base, nq)], kv.at[pl.ds(base, nq)], g_s.at[k - 1], g_r.at[k - 1], at_x(k))
-        for k in range(1, nx)
+        remote(send_g, recv_g.at[k - 1], g_s.at[k - 1], g_r.at[k - 1], at_x(k)) for k in range(1, nx)
     ]
     for copy in g_copies:
         copy.start()
     b_copies = all_z(lambda t: send_b.at[t], recv_b.at[z], b_s, b_r, True)
     u_copy = remote(upk, upair, u_s, u_r, (dp, x * nz + lax.div(z, 2) * 2 + 1 - odd))
     u_copy.start()
-    own = pltpu.roll(kv[pl.ds(base, nq), :].astype(F32), 256 - HEAD_DIM, 1)
-    lanes = lane_iota(nq, 256)
-    own = jnp.where((lanes >= HEAD_DIM) & (lanes < 2 * HEAD_DIM), own, 0.0)
-    q_zero[...] = own.astype(BF16)
-    q_mask[...] = jnp.where(lanes == 240, FAR, own).astype(BF16)
+    for copy in b_copies:
+        copy.wait()
+    for p in range(sz.pairs):
+        both = recv_b[2 * p].astype(F32) + recv_b[2 * p + 1].astype(F32)
+        main, rest = both[0:cap, :], unfold(both[cap:, :])
+        at = slice(p * cap, (p + 1) * cap)
+        query = jnp.concatenate(
+            [jnp.zeros((cap, 80), F32), main[:, 0:80], jnp.zeros((cap, 96), F32)], axis=1
+        )
+        q_zero[at, :] = query.astype(BF16)
+        q_mask[at, :] = jnp.where(lane_iota(cap, 256) == 240, FAR, query).astype(BF16)
+        d_out[at, :] = jnp.concatenate(
+            [main[:, 80:128], rest[:, 0:32], jnp.zeros((cap, 176), F32)], axis=1
+        ).astype(BF16)
 
     def group(k):
         g = lax.rem(x + nx - k, nx)
@@ -192,16 +225,17 @@
 
     top = score_group(0, jnp.full((1, nq), -3e38, F32))
 
-    for copy in b_copies:
-        copy.wait()
-    d_out[...] = jnp.zeros_like(d_out)
-    for p in range(sz.pairs):
-        both = recv_b[2 * p].astype(F32) + recv_b[2 * p + 1].astype(F32)
-        d_out[p * cap : (p + 1) * cap, 0:128] = both.astype(BF16)
     d_out_t = nt(eye[0:HEAD_DIM, 0:128], d_out[:, 0:128])
 
     for k in range(1, nx):
         g_copies[k - 1].wait()
+        _, at = group(k)
+        for p in range(sz.pairs):
+            main = recv_g[k - 1, p * cap : (p + 1) * cap, :].astype(F32)
+            rest = recv_g[k - 1, nq:, :].astype(F32)[:, 32 * p : 32 * p + 32]
+            mask = jnp.broadcast_to(jnp.where(main[:, 0:1] > DEAD / 2, -1.0, 0.0), (cap, 96))
+            start = pl.multiple_of(at.start + p * cap, 16)
+            kv[pl.ds(start, cap), :] = jnp.concatenate([main, rest, mask], axis=1).astype(BF16)
         top = score_group(k, top)
 
     total = jnp.zeros((1, nq), F32)
@@ -252,15 +286,26 @@
         w = (e * inverse).astype(BF16)
         grad_prob = nt(kv[at, :], d_out[...])
         ds = (e * slope * (grad_prob - delta)).astype(BF16)
-        dkv[at, :] = (nn(ds, q_zero[...]) + nn(w, d_out[...])).astype(BF16)
-        if k:
+        term = nn(ds, q_zero[...]) + nn(w, d_out[...])
+        if k == 0:
+            dkv[...] = term
+        else:
+            send_c[k - 1, 0:nq, :] = term[:, 0:128].astype(BF16)
+            send_c[k - 1, nq:, 0 : 32 * sz.pairs] = jnp.concatenate(
+                [term[p * cap : (p + 1) * cap, 128:160] for p in range(sz.pairs)], axis=1
+            ).astype(BF16)
             copy = remote(
-                dkv.at[at], recv_c.at[k - 1], c_s.at[k - 1], c_r.at[k - 1], (dp, g * nz + z)
+                send_c.at[k - 1], recv_c.at[k - 1], c_s.at[k - 1], c_r.at[k - 1], (dp, g * nz + z)
             )
             copy.start()
             c_copies.append(copy)
         dq_t = dq_t + nn(kvt[g, HEAD_DIM : 2 * HEAD_DIM, :], ds)
-    dq_t = dq_t.astype(BF16)
+    dq = nt(eye_q, dq_t.astype(BF16)).astype(BF16)
+    send_f[...] = jnp.zeros_like(send_f)
+    for p in range(sz.pairs):
+        send_f[p, :, 0:HEAD_DIM] = dq[p * cap : (p + 1) * cap, :]
+    f_copies = all_z(lambda t: send_f.at[lax.div(t, 2)], recv_f.at[z], f_s, f_r, True)
+    recv_f[z] = send_f[lax.div(z, 2)]
 
     u_copy.wait()
     upk_all = (upk[...].astype(F32) + upair[...].astype(F32)).astype(BF16)
@@ -288,11 +333,6 @@
     for i in range(ny):
         wown[i] = nn(terms[i], upair[:, own_cols])
 
-    dq = nt(eye_q, dq_t)
-    dq = jnp.concatenate(
-        [jnp.zeros((nq, 2 * HEAD_DIM), F32), dq, jnp.zeros((nq, 16), F32)], axis=1
-    )
-
     w1.wait()
 
     for i in range(ny):
@@ -309,12 +349,15 @@
 
     for copy in c_copies:
         copy.wait()
-    mine = dkv[pl.ds(base, nq), :].astype(F32) + dq
+    mine, rest = dkv[:, 0:128], jnp.zeros((cap, 128), F32)
     for k in range(1, nx):
-        mine = mine + recv_c[k - 1].astype(F32)
-    mine = mine.astype(BF16)
+        mine = mine + recv_c[k - 1, 0:nq, :].astype(F32)
+        rest = rest + recv_c[k - 1, nq:, :].astype(F32)
     for p in range(sz.pairs):
-        send_d[p] = mine[p * cap : (p + 1) * cap, :]
+        at = slice(p * cap, (p + 1) * cap)
+        tail = dkv[at, 128:160] + rest[:, 32 * p : 32 * p + 32]
+        send_d[p, 0:cap, :] = mine[at, :].astype(BF16)
+        send_d[p, cap:, :] = fold(jnp.concatenate([tail, jnp.zeros((cap, 8), F32)], axis=1)).astype(BF16)
     d_copies = all_z(lambda t: send_d.at[lax.div(t, 2)], recv_d.at[z], d_s, d_r, True)
     recv_d[z] = send_d[lax.div(z, 2)]
 
@@ -338,17 +381,23 @@
     for copy in w3:
         copy.start()
 
-    for copy in d_copies:
-        copy.wait()
     stores = []
-    for t, dst in enumerate((gv_hbm, gk_hbm, gq_hbm)):
-        at = t * HEAD_DIM
-        merged = jnp.concatenate(
-            [recv_d[h].astype(F32)[:, at : at + HEAD_DIM] for h in range(heads)], axis=1
-        ).astype(BF16)
+
+    def give(t, dst, parts):
+        merged = jnp.concatenate(parts, axis=1).astype(BF16)
         stage[t] = nn(unpick, merged).astype(BF16)
         stores.append(pltpu.make_async_copy(stage.at[t], dst.at[0], store_sem.at[t]))
         stores[-1].start()
+
+    for copy in f_copies:
+        copy.wait()
+    give(0, gq_hbm, [recv_f[h].astype(F32)[:, 0:HEAD_DIM] for h in range(heads)])
+    for copy in d_copies:
+        copy.wait()
+    mains = [recv_d[h, 0:cap, :].astype(F32) for h in range(heads)]
+    rests = [unfold(recv_d[h, cap:, :].astype(F32))[:, 0:32] for h in range(heads)]
+    give(1, gv_hbm, [m[:, 0:HEAD_DIM] for m in mains])
+    give(2, gk_hbm, [m for h in range(heads) for m in (mains[h][:, HEAD_DIM:], rests[h])])
 
     for copy in w3:
         copy.wait()
@@ -465,19 +514,22 @@
     nx, nz, ny, cap, heads = sz.nx, sz.nz, sz.ny, sz.cap, sz.heads
     nq, nk, hd, width, rows = sz.queries, sz.keys, sz.hd, sz.width, sz.rows
     half, share, pairs = sz.half, sz.share, sz.pairs
+    long, wide = cap + cap // 3, nq + cap
     hbm = pl.BlockSpec(memory_space=pl.ANY)
     vmem = pl.BlockSpec(memory_space=pltpu.VMEM)
     grad = jax.ShapeDtypeStruct((1, rows, hd), BF16)
     dma = pltpu.SemaphoreType.DMA
     buffers = [
         ((rows, hd), BF16), ((rows, hd), BF16), ((rows, hd), BF16), ((rows, width), BF16), ((hd, width), BF16),
-        ((heads, cap, 256), BF16), ((heads, cap, 256), BF16),
-        ((heads, cap, 128), BF16), ((heads, cap, 128), BF16),
+        ((heads, long, 128), BF16), ((heads, long, 128), BF16),
+        ((heads, long, 128), BF16), ((heads, long, 128), BF16),
+        ((wide, 128), BF16), ((nx - 1, wide, 128), BF16),
         ((nk, 256), BF16), ((nx, 256, nq), BF16), ((nq, 256), BF16), ((nq, 256), BF16), ((nq, 256), BF16),
         ((nk, nq), F32),
         ((pairs, cap, 128), BF16), ((ny, cap, 128), BF16),
-        ((nk, 256), BF16), ((nx - 1, nq, 256), BF16),
-        ((sz.pairs, cap, 256), BF16), ((heads, cap, 256), BF16),
+        ((nq, 256), F32), ((nx - 1, wide, 128), BF16), ((nx - 1, wide, 128), BF16),
+        ((pairs, cap, 128), BF16), ((heads, cap, 128), BF16),
+        ((pairs, long, 128), BF16), ((heads, long, 128), BF16),
         ((cap, width), BF16), ((cap, width), BF16),
         ((ny, HEAD_DIM, half), F32), ((ny, HEAD_DIM, half), BF16), ((ny, HEAD_DIM, half), BF16),
         ((ny, HEAD_DIM, half), BF16), ((ny - 1, HEAD_DIM, half), BF16),
@@ -489,7 +541,7 @@
     ]
     zs, xs, ys, ps, one = dma((nz - 1,)), dma((nx - 1,)), dma((ny - 1,)), dma((pairs,)), dma
     scratch = [pltpu.VMEM(shape, kind) for shape, kind in buffers]
-    scratch += [dma((5,)), dma((3,)), one, one]
+    scratch += [dma((5,)), dma((3,)), one, one, zs, zs]
     scratch += [zs, zs, zs, zs, xs, xs, ps, dma((ny,)), xs, xs, zs, zs]
     scratch += [one, one, ys, ys, dma((pairs - 1,)), dma((pairs - 1,)), xs, xs]
     scratch += [dma((sz.per_head,)), ps, dma((2 * ny - 1,)), dma((2,))]

time: 101 us -> 86.1 us (0.85)
  Pallas kernels: 96.1 us -> 80.9 us
    pallas_call x1, Pallas kernels: 96.1 us -> 80.9 us  [per_device(): pl.pallas_call(functools.partial(kernel, sz), out_shape=(grad, grad, grad...]
where the time goes in v3:
time: 86.1 us; the launch traced here: 85.9 us
  Pallas kernels  80.9 us (94%)
  local copies, waits for them, and re-layouts  4.41 us (5%)
    pallas_call x1, Pallas kernels, per_device(): pl.pallas_call(functools.partial(kernel, sz), out_shape=(grad, grad, grad...  80.9 us
    unnamed x10, local copies, waits for them, and re-layouts  4.41 us

profile of v3, /device:TPU:17, one launch (start us, length us, event | category | flops | bytes accessed | tf_op | source)
XLA Modules:
  0.0 85.9 jit_solution(10015069972716569154)
XLA Ops:
  0.6 80.9 %shard_map.93 = (bf16[1,512,640]{2,1,0:T(8,128)(2,1)}, bf16[1,512,640]{2,1,0:T(8,128)(2,1)}, bf16[1,512,640]{2,1,0:T(8,128)(2,1)}, f32[20,1280]{1,0:T(8,128)}) custom-call(s32[1,512]{1,0:T(1,128)} %vis_ref.1, bf16[1,512,640]{2,1,0:T(8,128)(2,1)} %q_hbm.1, bf16[1,512,640]{2,1,0:T(8,128)(2,1)} %k_hbm.1, bf16[1,512,640]{2,1,0:T(8,128)(2,1)} %v_hbm.1, ...), custom_call_target="tpu_custom_call" | custom-call | tf_op jit(solution)/shard_map/pallas_call | solution.py:548
  81.5 0.0 copy-start.1
  81.5 0.0 copy-start
  81.5 2.1 %copy.14 = bf16[1,512,640]{2,1,0:T(8,128)(2,1)} copy(bf16[1,512,640]{2,1,0:T(8,128)(2,1)} %get-tuple-element.8) | data formatting | bytes 1310720
  83.6 0.0 copy-done.1
  83.6 0.0 copy-start.2
  83.6 0.8 copy.15
  84.4 0.0 copy-done
  84.5 0.8 copy.16
  85.3 0.0 copy-done.2
  85.3 0.6 copy.17
Async XLA Ops:
  81.5 2.1 %copy-start.1 = (bf16[1,512,640]{2,1,0:T(8,128)(2,1)S(1)}, bf16[1,512,640]{2,1,0:T(8,128)(2,1)}, u32[]{:S(2)}) copy-start(bf16[1,512,640]{2,1,0:T(8,128)(2,1)} %get-tuple-element.9) | copy-start | bytes 1966084
  81.5 2.9 %copy-start = (bf16[1,512,640]{2,1,0:T(8,128)(2,1)S(1)}, bf16[1,512,640]{2,1,0:T(8,128)(2,1)}, u32[]{:S(2)}) copy-start(bf16[1,512,640]{2,1,0:T(8,128)(2,1)} %get-tuple-element.10) | copy-start | bytes 1966084
  83.6 1.7 %copy-start.2 = (f32[20,1280]{1,0:T(8,128)S(1)}, f32[20,1280]{1,0:T(8,128)}, u32[]{:S(2)}) copy-start(f32[20,1280]{1,0:T(8,128)} %get-tuple-element.11) | copy-start | bytes 307204

commit v4 on v3

--- a/solution.py
+++ b/solution.py
@@ -66,7 +66,7 @@
 def kernel(
     sz,
     vis_ref, q_hbm, k_hbm, v_hbm, u_hbm, w_hbm,
-    gq_hbm, gk_hbm, gv_hbm, gw_ref,
+    grads_hbm, gw_ref,
     qin, kin, vin, uin, win,
     send_a, recv_a, send_b, recv_b,
     send_g, recv_g, kv, kvt, q_mask, q_zero, d_out, scores,
@@ -195,9 +195,9 @@
         copy.start()
     b_copies = all_z(lambda t: send_b.at[t], recv_b.at[z], b_s, b_r, True)
     u_copy = remote(upk, upair, u_s, u_r, (dp, x * nz + lax.div(z, 2) * 2 + 1 - odd))
+    for copy in b_copies:
+        copy.wait()
     u_copy.start()
-    for copy in b_copies:
-        copy.wait()
     for p in range(sz.pairs):
         both = recv_b[2 * p].astype(F32) + recv_b[2 * p + 1].astype(F32)
         main, rest = both[0:cap, :], unfold(both[cap:, :])
@@ -347,20 +347,6 @@
     for copy in w2:
         copy.start()
 
-    for copy in c_copies:
-        copy.wait()
-    mine, rest = dkv[:, 0:128], jnp.zeros((cap, 128), F32)
-    for k in range(1, nx):
-        mine = mine + recv_c[k - 1, 0:nq, :].astype(F32)
-        rest = rest + recv_c[k - 1, nq:, :].astype(F32)
-    for p in range(sz.pairs):
-        at = slice(p * cap, (p + 1) * cap)
-        tail = dkv[at, 128:160] + rest[:, 32 * p : 32 * p + 32]
-        send_d[p, 0:cap, :] = mine[at, :].astype(BF16)
-        send_d[p, cap:, :] = fold(jnp.concatenate([tail, jnp.zeros((cap, 8), F32)], axis=1)).astype(BF16)
-    d_copies = all_z(lambda t: send_d.at[lax.div(t, 2)], recv_d.at[z], d_s, d_r, True)
-    recv_d[z] = send_d[lax.div(z, 2)]
-
     for copy in w2:
         copy.wait()
     red[...] = wown[y]
@@ -381,23 +367,27 @@
     for copy in w3:
         copy.start()
 
+    for copy in c_copies:
+        copy.wait()
+    mine, rest = dkv[:, 0:128], jnp.zeros((cap, 128), F32)
+    for k in range(1, nx):
+        mine = mine + recv_c[k - 1, 0:nq, :].astype(F32)
+        rest = rest + recv_c[k - 1, nq:, :].astype(F32)
+    for p in range(sz.pairs):
+        at = slice(p * cap, (p + 1) * cap)
+        tail = dkv[at, 128:160] + rest[:, 32 * p : 32 * p + 32]
+        send_d[p, 0:cap, :] = mine[at, :].astype(BF16)
+        send_d[p, cap:, :] = fold(jnp.concatenate([tail, jnp.zeros((cap, 8), F32)], axis=1)).astype(BF16)
+    d_copies = all_z(lambda t: send_d.at[lax.div(t, 2)], recv_d.at[z], d_s, d_r, True)
+    recv_d[z] = send_d[lax.div(z, 2)]
+
     stores = []
 
     def give(t, dst, parts):
         merged = jnp.concatenate(parts, axis=1).astype(BF16)
         stage[t] = nn(unpick, merged).astype(BF16)
-        stores.append(pltpu.make_async_copy(stage.at[t], dst.at[0], store_sem.at[t]))
+        stores.append(pltpu.make_async_copy(stage.at[t], dst, store_sem.at[t]))
         stores[-1].start()
-
-    for copy in f_copies:
-        copy.wait()
-    give(0, gq_hbm, [recv_f[h].astype(F32)[:, 0:HEAD_DIM] for h in range(heads)])
-    for copy in d_copies:
-        copy.wait()
-    mains = [recv_d[h, 0:cap, :].astype(F32) for h in range(heads)]
-    rests = [unfold(recv_d[h, cap:, :].astype(F32))[:, 0:32] for h in range(heads)]
-    give(1, gv_hbm, [m[:, 0:HEAD_DIM] for m in mains])
-    give(2, gk_hbm, [m for h in range(heads) for m in (mains[h][:, HEAD_DIM:], rests[h])])
 
     for copy in w3:
         copy.wait()
@@ -443,6 +433,10 @@
             def _():
                 wrecv5[lax.div(z, 2)] = wsend5[...]
 
+    for copy in f_copies:
+        copy.wait()
+    give(0, grads_hbm.at[0], [recv_f[h].astype(F32)[:, 0:HEAD_DIM] for h in range(heads)])
+
     block = lax.div(seq, per_head)
     owner = y == lax.rem(block, ny)
     w6 = [
@@ -480,6 +474,16 @@
 
         for copy in w6:
             copy.start()
+
+    for copy in d_copies:
+        copy.wait()
+    give(1, grads_hbm.at[2], [recv_d[h, 0:cap, :].astype(F32)[:, 0:HEAD_DIM] for h in range(heads)])
+
+    keys_parts = []
+    for h in range(heads):
+        keys_parts.append(recv_d[h, 0:cap, :].astype(F32)[:, HEAD_DIM:])
+        keys_parts.append(unfold(recv_d[h, cap:, :].astype(F32))[:, 0:32])
+    give(2, grads_hbm.at[1], keys_parts)
 
     @pl.when(jnp.logical_not(owner))
     def _():
@@ -517,7 +521,7 @@
     long, wide = cap + cap // 3, nq + cap
     hbm = pl.BlockSpec(memory_space=pl.ANY)
     vmem = pl.BlockSpec(memory_space=pltpu.VMEM)
-    grad = jax.ShapeDtypeStruct((1, rows, hd), BF16)
+    grad = jax.ShapeDtypeStruct((3, rows, hd), BF16)
     dma = pltpu.SemaphoreType.DMA
     buffers = [
         ((rows, hd), BF16), ((rows, hd), BF16), ((rows, hd), BF16), ((rows, width), BF16), ((hd, width), BF16),
@@ -545,16 +549,17 @@
     scratch += [zs, zs, zs, zs, xs, xs, ps, dma((ny,)), xs, xs, zs, zs]
     scratch += [one, one, ys, ys, dma((pairs - 1,)), dma((pairs - 1,)), xs, xs]
     scratch += [dma((sz.per_head,)), ps, dma((2 * ny - 1,)), dma((2,))]
-    return pl.pallas_call(
+    grads, weight = pl.pallas_call(
         functools.partial(kernel, sz),
-        out_shape=(grad, grad, grad, jax.ShapeDtypeStruct((sz.out_rows, width), F32)),
+        out_shape=(grad, jax.ShapeDtypeStruct((sz.out_rows, width), F32)),
         in_specs=[vmem] + [hbm] * 5,
-        out_specs=(hbm, hbm, hbm, vmem),
+        out_specs=(hbm, vmem),
         scratch_shapes=scratch,
         compiler_params=pltpu.CompilerParams(
             collective_id=0, has_side_effects=True, vmem_limit_bytes=56 * 1024 * 1024
         ),
     )(visible, queries, keys, values, upstream, out_weight)
+    return grads[0:1], grads[1:2], grads[2:3], weight
 
 
 def build(mesh, nz, ny, cap):

time: 86.1 us -> 82.9 us (0.963)
  Pallas kernels: 80.9 us -> 78.6 us
  local copies, waits for them, and re-layouts: 4.41 us -> 3.49 us
    unnamed x10 -> x3, local copies, waits for them, and re-layouts: 4.41 us -> 0.65 us
    slice x0 -> x1, local copies, waits for them, and re-layouts: none -> 2.84 us  [per_device(): return (grads[0:1], grads[1:2], grads[2:3], weight)]
    pallas_call x1, Pallas kernels: 80.9 us -> 78.6 us  [per_device(): pl.pallas_call(functools.partial(kernel, sz), out_shape=(grad, jax.ShapeD...]
where the time goes in v4:
time: 82.9 us; the launch traced here: 82.8 us
  Pallas kernels  78.6 us (95%)
  local copies, waits for them, and re-layouts  3.49 us (4%)
    pallas_call x1, Pallas kernels, per_device(): pl.pallas_call(functools.partial(kernel, sz), out_shape=(grad, jax.ShapeD...  78.6 us
    slice x1, local copies, waits for them, and re-layouts, per_device(): return (grads[0:1], grads[1:2], grads[2:3], weight)  2.84 us

profile of v4, /device:TPU:17, one launch (start us, length us, event | category | flops | bytes accessed | tf_op | source)
XLA Modules:
  0.0 82.8 jit_solution(15996960831585011398)
XLA Ops:
  0.6 78.6 %shard_map.93 = (bf16[3,512,640]{2,1,0:T(8,128)(2,1)}, f32[20,1280]{1,0:T(8,128)}) custom-call(s32[1,512]{1,0:T(1,128)} %vis_ref.1, bf16[1,512,640]{2,1,0:T(8,128)(2,1)} %q_hbm.1, bf16[1,512,640]{2,1,0:T(8,128)(2,1)} %k_hbm.1, bf16[1,512,640]{2,1,0:T(8,128)(2,1)} %v_hbm.1, bf16[1,512,1280]{2,1,0:T(8,128)(2,1)} %u_hbm.1, bf16[640,1280]{1,0:T(8,128)(2,1)} %w_hbm.1), custom_call_target="tpu_custom_call" | custom-call | tf_op jit(solution)/shard_map/pallas_call | solution.py:552
  79.3 0.0 copy-start
  79.3 2.8 %fusion = (bf16[1,512,640]{2,1,0:T(8,128)(2,1)}, bf16[1,512,640]{2,1,0:T(8,128)(2,1)}, bf16[1,512,640]{2,1,0:T(8,128)(2,1)}) fusion(bf16[3,512,640]{2,1,0:T(8,128)(2,1)} %get-tuple-element.6), kind=kLoop, calls=%fused_computation | loop fusion | bytes 3932160 | tf_op jit(solution)/shard_map/slice | solution.py:562
  82.1 0.0 copy-done
  82.1 0.6 copy.11
Async XLA Ops:
  79.3 2.9 %copy-start = (f32[20,1280]{1,0:T(8,128)S(1)}, f32[20,1280]{1,0:T(8,128)}, u32[]{:S(2)}) copy-start(f32[20,1280]{1,0:T(8,128)} %get-tuple-element.18) | copy-start | bytes 307204

commit v5 on v4

--- a/solution.py
+++ b/solution.py
@@ -117,7 +117,8 @@
     ):
         source = src.at[0] if i < 4 else src
         loads.append(pltpu.make_async_copy(source, dst, load_sem.at[i]))
-        loads[-1].start()
+        if i < 2:
+            loads[-1].start()
 
     seen = vis_ref[...].astype(F32)
     rows = sz.rows
@@ -136,6 +137,8 @@
 
     loads[0].wait()
     loads[1].wait()
+    for load in loads[2:]:
+        load.start()
     pv, pk = nn(pick, vin[...]), nn(pick, kin[...])
     flags = jnp.broadcast_to(live, (cap, 8))
 
@@ -172,6 +175,10 @@
     recv_a[z] = send_a[z]
     recv_b[z] = send_b[z]
     eye = identity(256)
+    eye_q = identity(nq)
+    send_e[...] = jnp.zeros_like(send_e)
+    send_f[...] = jnp.zeros_like(send_f)
+    tiles[...] = jnp.zeros_like(tiles)
     unpick = nt(identity(rows), pick).astype(BF16)
 
     for copy in a_copies:
@@ -252,8 +259,6 @@
         w = (scores[at, :] * inverse).astype(BF16)
         attended_t = attended_t + nn(kvt[g, 0:HEAD_DIM, :], w)
     attended_t = attended_t.astype(BF16)
-    eye_q = identity(nq)
-    send_e[...] = jnp.zeros_like(send_e)
     attended = nt(eye_q, attended_t).astype(BF16)
     for p in range(sz.pairs):
         send_e[p, :, 0:HEAD_DIM] = attended[p * cap : (p + 1) * cap, :]
@@ -301,7 +306,6 @@
             c_copies.append(copy)
         dq_t = dq_t + nn(kvt[g, HEAD_DIM : 2 * HEAD_DIM, :], ds)
     dq = nt(eye_q, dq_t.astype(BF16)).astype(BF16)
-    send_f[...] = jnp.zeros_like(send_f)
     for p in range(sz.pairs):
         send_f[p, :, 0:HEAD_DIM] = dq[p * cap : (p + 1) * cap, :]
     f_copies = all_z(lambda t: send_f.at[lax.div(t, 2)], recv_f.at[z], f_s, f_r, True)
@@ -352,7 +356,6 @@
     red[...] = wown[y]
     for k in range(1, ny):
         red[...] = red[...] + wrecv2[k - 1].astype(F32)
-    tiles[...] = jnp.zeros_like(tiles)
     for r in range(HEAD_DIM // 16):
         for c in range(sz.col_tiles):
             tiles[r * sz.col_tiles + c] = red[16 * r : 16 * r + 16, 128 * c : 128 * c + 128].astype(BF16)

time: 82.9 us -> 82.9 us (level)
  no operation moved by 1% of the time
where the time goes in v5:
time: 82.9 us; the launch traced here: 82.7 us
  Pallas kernels  78.6 us (95%)
  local copies, waits for them, and re-layouts  3.49 us (4%)
    pallas_call x1, Pallas kernels, per_device(): pl.pallas_call(functools.partial(kernel, sz), out_shape=(grad, jax.ShapeD...  78.6 us
    slice x1, local copies, waits for them, and re-layouts, per_device(): return (grads[0:1], grads[1:2], grads[2:3], weight)  2.84 us

profile of v5, /device:TPU:17, one launch (start us, length us, event | category | flops | bytes accessed | tf_op | source)
XLA Modules:
  0.0 82.7 jit_solution(4759967277600763145)
XLA Ops:
  0.6 78.6 %shard_map.93 = (bf16[3,512,640]{2,1,0:T(8,128)(2,1)}, f32[20,1280]{1,0:T(8,128)}) custom-call(s32[1,512]{1,0:T(1,128)} %vis_ref.1, bf16[1,512,640]{2,1,0:T(8,128)(2,1)} %q_hbm.1, bf16[1,512,640]{2,1,0:T(8,128)(2,1)} %k_hbm.1, bf16[1,512,640]{2,1,0:T(8,128)(2,1)} %v_hbm.1, bf16[1,512,1280]{2,1,0:T(8,128)(2,1)} %u_hbm.1, bf16[640,1280]{1,0:T(8,128)(2,1)} %w_hbm.1), custom_call_target="tpu_custom_call" | custom-call | tf_op jit(solution)/shard_map/pallas_call | solution.py:555
  79.2 0.0 copy-start
  79.2 2.8 %fusion = (bf16[1,512,640]{2,1,0:T(8,128)(2,1)}, bf16[1,512,640]{2,1,0:T(8,128)(2,1)}, bf16[1,512,640]{2,1,0:T(8,128)(2,1)}) fusion(bf16[3,512,640]{2,1,0:T(8,128)(2,1)} %get-tuple-element.6), kind=kLoop, calls=%fused_computation | loop fusion | bytes 3932160 | tf_op jit(solution)/shard_map/slice | solution.py:565
  82.1 0.0 copy-done
  82.1 0.6 copy.11
Async XLA Ops:
  79.2 2.9 %copy-start = (f32[20,1280]{1,0:T(8,128)S(1)}, f32[20,1280]{1,0:T(8,128)}, u32[]{:S(2)}) copy-start(f32[20,1280]{1,0:T(8,128)} %get-tuple-element.18) | copy-start | bytes 307204
